TPU v7x, 128 devices: a whole 4x4x4 slice. The times are simulated.
128 devices in a mesh: dom: 16 (over z, y_hi, core), rot: 8 (over y_lo, x).
Axes of the slice: x: 4, y: 4 (y_hi: 2, y_lo: 2; y = y_hi * 2 + y_lo), z: 4, core: 2. Of those that a mesh axis runs over, the one named last changes fastest.
Arguments:
- particles: bfloat16 [128, 64, 4096], P('dom'), may hold values from -6 to 6
- references: bfloat16 [32, 64, 4096], P('rot', 'dom'), may hold values from -6 to 6
- part_class: int32 [128, 1], P('dom'), may hold values from 0 to 7; in each aligned block of 8 rows (0 to 7, 8 to 15, ...) at most 4 rows name the same one
- part_rot: int32 [128], P('dom'), may hold values from 0 to 3
- bucket: int32 [128], P('dom'), may hold values from 0 to 7
- bucket_weights: bfloat16 [8], replicated, may hold values from 0.25 to 2
- live_count: int32 [16], P('dom'), may hold values from 4 to 8, as said below
Outputs:
- scores: float32 [128, 512], P('dom')
- sums: float32 [64, 32, 64, 128], P('dom', 'rot')
Inputs may be any that keep to these rules, and one draw needn't show every extreme that they name: `part_class`: among the 8 particles of one index of dom no class is named more than 4 times, and some class is named 4 times in some such block. `live_count`: some block has all 8 particles in use.
All inputs are finite; a program needn't handle non-finite values.
Results may differ from a plain program's by a relative error of at most 0.014.
Values may be sent and summed in bfloat16 or wider, within the bound.
No kernel may reach another device: no remote copies, remote signals or barrier semaphores. Data moves between devices by JAX's collectives and lax.ppermute only.
A program may use at most 192 MiB of HBM per device.

v0:
```python
import math

import jax
import jax.numpy as jnp
import numpy as np
from jax import lax
from jax.experimental import pallas as pl
from jax.experimental.pallas import tpu as pltpu
from jax.sharding import PartitionSpec as P

BOX = 64
SHIFTS = 8
ROT_CLS = 4
CAP = 4
HALF = 33
KXP = 48
KXV = 40
PAIRS = BOX // 2
DOM = 16
BF = jnp.bfloat16
F32 = jnp.float32


def grid_cos_sin(rows, cols):
    theta = ((rows[:, None] * cols[None, :]) % BOX).astype(np.float64) * (2.0 * math.pi / BOX)
    return np.cos(theta), np.sin(theta)


def x_half_table():
    c, s = grid_cos_sin(np.arange(BOX), np.arange(BOX))
    out = np.zeros((2, KXP, BOX))
    out[0, :HALF] = c[:HALF]
    out[1, :HALF] = -s[:HALF]
    return out.reshape(2 * KXP, BOX)


def z_complex_table():
    c, s = grid_cos_sin(np.arange(BOX), np.arange(BOX))
    two = np.eye(2)
    return np.block([[np.kron(two, c), np.kron(two, -s)], [np.kron(two, s), np.kron(two, c)]])


def shift_tables():
    c, s = grid_cos_sin(np.arange(SHIFTS) - SHIFTS // 2, np.arange(BOX))
    fold = np.zeros((KXV,))
    fold[:HALF] = 2.0
    fold[0] = fold[HALF - 1] = 1.0
    ex = np.zeros((2 * SHIFTS, KXV))
    ex[:SHIFTS, :HALF] = c[:, :HALF]
    ex[SHIFTS:, :HALF] = s[:, :HALF]
    ex = ex * fold[None, :]
    wz = np.zeros((2, 4 * BOX, 128))
    wz[0, :, :SHIFTS] = np.concatenate([c.T, c.T, -s.T, -s.T], axis=0)
    wz[1, :, :SHIFTS] = np.concatenate([-s.T, -s.T, -c.T, -c.T], axis=0)
    return ex, wz.reshape(8 * BOX, 128)


def z_real_table():
    c, s = grid_cos_sin(np.arange(BOX), np.arange(BOX))
    return np.kron(np.eye(2), np.concatenate([c, -s], axis=1))


def y_table(rows):
    c, s = grid_cos_sin(np.arange(BOX), np.arange(BOX))
    order = np.concatenate([np.arange(0, BOX, 2), np.arange(1, BOX, 2)])
    both = np.concatenate([c[:, order], s[:, order]], axis=0)
    return np.kron(both, np.eye(rows))


def x_rows_table():
    c, s = grid_cos_sin(np.arange(BOX), np.arange(BOX))
    full = []
    for table in (c, s):
        spread = np.einsum(
            "rq,kdx->rkdqx", np.eye(ROT_CLS), table.reshape(BOX, DOM, BOX // DOM)
        ).reshape(ROT_CLS * BOX, ROT_CLS * BOX)
        high = spread.astype(np.float32).astype(BF)
        low = (spread.astype(np.float32) - high.astype(np.float32)).astype(BF)
        full += [high, low]
    return np.stack(full)


def z_stage(src, table, start, count):
    parts = []
    for j in range(start, start + count):
        lanes = slice(128 * j, 128 * (j + 1))
        parts.append(jnp.concatenate([src[0:KXP, lanes], src[KXP : 2 * KXP, lanes]], axis=1))
    return jnp.dot(jnp.concatenate(parts, axis=0), table, preferred_element_type=F32)


STEP = 8


def particle_kernel(count_ref, xp_ref, table_ref, out_ref):
    @pl.when(pl.program_id(0) < count_ref[0])
    def _():
        table = table_ref[...]
        for start in range(0, PAIRS, STEP):
            part = z_stage(xp_ref, table, start, STEP)
            out_ref[start * KXP : (start + STEP) * KXP, :] = part.astype(BF)

    @pl.when(pl.program_id(0) >= count_ref[0])
    def _():
        out_ref[...] = jnp.zeros_like(out_ref)


def score_kernel(count_ref, zp_ref, xr_ref, table_ref, ex_ref, wz_ref, out_ref, p_s, r_s, o_s, a_s):
    @pl.when(pl.program_id(0) < count_ref[0])
    def _():
        table = table_ref[...]
        for start in range(0, PAIRS, STEP):
            part = z_stage(xr_ref, table, start, STEP)
            part = part.astype(BF).astype(F32).reshape(STEP, KXP, 4 * BOX)
            r_s[start : start + STEP] = part[:, :KXV, :]
            mine = zp_ref[start * KXP : (start + STEP) * KXP, :].astype(F32)
            p_s[start : start + STEP] = mine.reshape(STEP, KXP, 4 * BOX)[:, :KXV, :]
        first = lax.broadcasted_iota(jnp.int32, (KXV, 128), 1) < BOX
        for j in range(PAIRS):
            for half in range(2):
                lanes = slice(128 * half, 128 * (half + 1))
                now = r_s[j, :, lanes]
                before = r_s[(j - 1) % PAIRS, :, lanes]
                o_s[j, :, lanes] = pltpu.roll(jnp.where(first, now, before), BOX, 1)

        def column(col, carry):
            rows = pl.ds(pl.multiple_of(col * 8, 8), 8)
            re = [jnp.zeros((8, 128), F32) for _ in range(SHIFTS)]
            im = [jnp.zeros((8, 128), F32) for _ in range(SHIFTS)]
            for j in range(PAIRS):
                pr = p_s[j, rows, 0:128]
                pi = p_s[j, rows, 128:256]
                for u in range(-2, 2):
                    m = (j - u) % PAIRS
                    for odd, src in ((0, r_s), (1, o_s)):
                        t = 2 * u + odd + SHIFTS // 2
                        rr = src[m, rows, 0:128]
                        ri = src[m, rows, 128:256]
                        re[t] = re[t] + (pr * rr + pi * ri)
                        im[t] = im[t] + (pi * rr - pr * ri)
            for t in range(SHIFTS):
                a_s[t, rows, 0:128] = re[t]
                a_s[t, rows, 128:256] = im[t]
            return carry

        lax.fori_loop(0, KXV // 8, column, 0)
        ex = ex_ref[...]
        along_x = [
            jnp.dot(ex, a_s[t].astype(BF), preferred_element_type=F32) for t in range(SHIFTS)
        ]
        cos_rows = jnp.concatenate([u[:SHIFTS] for u in along_x], axis=0).astype(BF)
        sin_rows = jnp.concatenate([u[SHIFTS:] for u in along_x], axis=0).astype(BF)
        both = jnp.concatenate([cos_rows, sin_rows], axis=1)
        final = jnp.dot(both, wz_ref[...], preferred_element_type=F32)
        out_ref[...] = final * (float(BOX) ** -3.5)

    @pl.when(pl.program_id(0) >= count_ref[0])
    def _():
        out_ref[...] = jnp.zeros_like(out_ref)


def yz_kernel(*refs):
    own_ref, part_refs, (z_ref, y_ref, out_ref) = refs[0], refs[1:8], refs[8:]
    total = own_ref[...].astype(F32)
    for part in part_refs:
        total = total + part[...].astype(F32)
    total = total.astype(BF)
    stacked = jnp.concatenate([total[:, 128 * j : 128 * (j + 1)] for j in range(PAIRS)], axis=0)
    z_part = jnp.dot(stacked, z_ref[...], preferred_element_type=F32).astype(BF)
    z_part = jnp.concatenate([z_part[:, :128], z_part[:, 128:]], axis=0)
    y_part = jnp.dot(y_ref[...], z_part, preferred_element_type=F32)
    half_rows = y_part.shape[0] // 2
    turned = pltpu.roll(y_part[half_rows:], BOX, 1)
    first = lax.broadcasted_iota(jnp.int32, turned.shape, 1) < BOX
    out_ref[...] = (y_part[:half_rows] + jnp.where(first, turned, -turned)).astype(BF)


def x_rows_kernel(rows_ref, table_ref, out_ref):
    rows = ROT_CLS * (BOX // DOM)
    first = lax.broadcasted_iota(jnp.int32, (ROT_CLS * BOX, 128), 1) < BOX
    for ky in range(BOX // DOM):
        grid = rows_ref[:, ky * rows : (ky + 1) * rows, :].reshape(ROT_CLS * BOX, 128)
        cos_part = jnp.dot(table_ref[0], grid, preferred_element_type=F32)
        cos_part = cos_part + jnp.dot(table_ref[1], grid, preferred_element_type=F32)
        sin_part = jnp.dot(table_ref[2], grid, preferred_element_type=F32)
        sin_part = sin_part + jnp.dot(table_ref[3], grid, preferred_element_type=F32)
        turned = pltpu.roll(sin_part, BOX, 1)
        total = (cos_part + jnp.where(first, turned, -turned)) * (float(BOX) ** -1.5)
        out_ref[ky] = total.reshape(ROT_CLS, BOX, 128)


VMEM = pl.BlockSpec(memory_space=pltpu.VMEM)
SMEM = pl.BlockSpec(memory_space=pltpu.SMEM)
PARAMS = pltpu.CompilerParams(vmem_limit_bytes=40 * 1024 * 1024)


def shards(particles, references, part_class, part_rot, bucket, bucket_weights, live_count):
    block_size = particles.shape[0]
    planes = references.shape[1]
    voxels = BOX * BOX
    dom = lax.axis_index("dom")
    owner = lax.axis_index("rot")
    chip, core = dom // 2, dom % 2

    all_refs = lax.all_gather(
        references.reshape(ROT_CLS * planes, voxels), "dom", axis=0, tiled=True
    )

    rows_all = jnp.arange(block_size, dtype=jnp.int32)
    classes = part_class[:, 0]
    alive = rows_all < live_count[0]
    same = (classes[:, None] == classes[None, :]) & alive[None, :]
    rank = jnp.sum((same & (rows_all[None, :] < rows_all[:, None])).astype(jnp.int32), axis=1)
    mine = (classes == owner) & alive
    count = jnp.sum(mine.astype(jnp.int32)).reshape(1)
    bucket_ids = jnp.arange(bucket_weights.shape[0], dtype=jnp.int32)
    level = jnp.where(
        bucket[:, None] == bucket_ids[None, :], bucket_weights[None, :].astype(F32), 0.0
    )
    weight = jnp.where(mine, jnp.sum(level, axis=1), 0.0)
    slot_ids = jnp.arange(CAP, dtype=jnp.int32)
    picked = (rank[None, :] == slot_ids[:, None]) & mine[None, :]
    slot_rot = jnp.sum(jnp.where(picked, part_rot[None, :], 0), axis=1)

    flat = particles.reshape(block_size * BOX, voxels)

    row = jnp.arange(DOM * ROT_CLS * planes, dtype=jnp.int32)
    row_x = row % planes
    row_r = (row // planes) % ROT_CLS
    row_chip = (row // (planes * ROT_CLS)) % 8
    row_core = row // (planes * ROT_CLS * 8)
    to_z = (chip // 2 + row_chip // 2) % 4
    to_y = (chip % 2) ^ (row_chip % 2)
    to_dom = (to_z * 2 + to_y) * 2 + (core ^ row_core)
    want_x = to_dom * planes + row_x
    col = jnp.arange(block_size * BOX, dtype=jnp.int32)
    col_weight = jnp.repeat(weight, BOX, total_repeat_length=block_size * BOX)
    col_rot = jnp.repeat(part_rot, BOX, total_repeat_length=block_size * BOX)
    spread = jnp.where(
        (want_x[:, None] == (col % BOX)[None, :]) & (row_r[:, None] == col_rot[None, :]),
        col_weight[None, :],
        0.0,
    ).astype(BF)
    to_send = jnp.dot(spread, flat, preferred_element_type=F32).astype(BF)
    half_rows = to_send.shape[0] // 2
    other = lax.ppermute(to_send[half_rows:], "dom", [(i, i ^ 1) for i in range(DOM)])
    pair_sum = (to_send[:half_rows].astype(F32) + other.astype(F32)).astype(BF)
    per_chip = ROT_CLS * planes
    arrived = []
    for k in range(1, 8):
        route = []
        for i in range(DOM):
            z, y, c = i // 4, (i // 2) % 2, i % 2
            route.append((i, ((z + k // 2) % 4) * 4 + (y ^ (k % 2)) * 2 + c))
        arrived.append(lax.ppermute(pair_sum[k * per_chip : (k + 1) * per_chip], "dom", route))

    z_real = jnp.asarray(z_real_table(), F32).astype(BF)
    y_full = jnp.asarray(y_table(per_chip).astype(BF))
    grids = pl.pallas_call(
        yz_kernel,
        out_shape=jax.ShapeDtypeStruct((BOX * per_chip, 2 * BOX), BF),
        in_specs=[VMEM] * 10,
        out_specs=VMEM,
        compiler_params=PARAMS,
        name="yz_planes",
    )(pair_sum[:per_chip], *arrived, z_real, y_full)
    by_rows = lax.all_to_all(grids, "dom", 0, 0, tiled=True)
    sums = pl.pallas_call(
        x_rows_kernel,
        out_shape=jax.ShapeDtypeStruct((BOX // DOM, ROT_CLS, BOX, 2 * BOX), F32),
        in_specs=[VMEM] * 2,
        out_specs=VMEM,
        compiler_params=PARAMS,
        name="x_rows",
    )(by_rows.reshape(DOM, BOX // DOM * per_chip, 2 * BOX), jnp.asarray(x_rows_table()))

    x_half = jnp.asarray(x_half_table().astype(BF))
    pick = (
        picked.astype(BF)[:, None, :, None] * x_half[None, :, None, :]
    ).reshape(CAP * 2 * KXP, block_size * BOX)
    along_x = jnp.dot(pick, flat, preferred_element_type=F32).astype(BF)
    z_table = jnp.asarray(z_complex_table().astype(BF))
    spectra = pl.pallas_call(
        particle_kernel,
        out_shape=jax.ShapeDtypeStruct((CAP, PAIRS * KXP, 4 * BOX), BF),
        grid=(CAP,),
        in_specs=[
            SMEM,
            pl.BlockSpec((None, 2 * KXP, voxels), lambda s: (s, 0, 0)),
            pl.BlockSpec((4 * BOX, 4 * BOX), lambda s: (0, 0)),
        ],
        out_specs=pl.BlockSpec((None, PAIRS * KXP, 4 * BOX), lambda s: (s, 0, 0)),
        compiler_params=PARAMS,
        name="particle_z",
    )(count, along_x.reshape(CAP, 2 * KXP, voxels), z_table)

    rot_ids = jnp.arange(ROT_CLS, dtype=jnp.int32)
    choose = (slot_rot[:, None] == rot_ids[None, :]).astype(BF)
    pick_ref = (
        choose[:, None, None, :, None] * x_half.reshape(1, 2 * KXP, DOM, 1, planes)
    ).reshape(CAP * 2 * KXP, DOM * per_chip)
    ref_x = jnp.dot(pick_ref, all_refs, preferred_element_type=F32).astype(BF)
    ex, wz = shift_tables()
    slots = pl.pallas_call(
        score_kernel,
        out_shape=jax.ShapeDtypeStruct((CAP, SHIFTS * SHIFTS, 128), F32),
        grid=(CAP,),
        in_specs=[
            SMEM,
            pl.BlockSpec((None, PAIRS * KXP, 4 * BOX), lambda s: (s, 0, 0)),
            pl.BlockSpec((None, 2 * KXP, voxels), lambda s: (s, 0, 0)),
            pl.BlockSpec((4 * BOX, 4 * BOX), lambda s: (0, 0)),
            pl.BlockSpec((2 * SHIFTS, KXV), lambda s: (0, 0)),
            pl.BlockSpec((8 * BOX, 128), lambda s: (0, 0)),
        ],
        out_specs=pl.BlockSpec((None, SHIFTS * SHIFTS, 128), lambda s: (s, 0, 0)),
        scratch_shapes=[
            pltpu.VMEM((PAIRS, KXV, 4 * BOX), F32),
            pltpu.VMEM((PAIRS, KXV, 4 * BOX), F32),
            pltpu.VMEM((PAIRS, KXV, 4 * BOX), F32),
            pltpu.VMEM((SHIFTS, KXV, 4 * BOX), F32),
        ],
        compiler_params=PARAMS,
        name="slot_scores",
    )(
        count,
        spectra,
        ref_x.reshape(CAP, 2 * KXP, voxels),
        z_table,
        jnp.asarray(ex.astype(BF)),
        jnp.asarray(wz.astype(BF)),
    )
    slot_scores = slots[:, :, :SHIFTS].reshape(CAP, SHIFTS, SHIFTS, SHIFTS)
    slot_scores = slot_scores.transpose(0, 2, 1, 3).reshape(CAP, SHIFTS**3)
    everywhere = lax.all_to_all(
        jnp.tile(slot_scores, (8, 1)), "rot", 0, 0, tiled=True
    )
    place = classes * CAP + rank
    found = (place[:, None] == jnp.arange(8 * CAP, dtype=jnp.int32)[None, :]) & alive[:, None]
    scores = jnp.sum(jnp.where(found[:, :, None], everywhere[None, :, :], 0.0), axis=1)
    return (scores, sums)


def solution(mesh):
    return jax.shard_map(
        shards,
        mesh=mesh,
        in_specs=(
            P("dom", None, None),
            P("rot", "dom", None),
            P("dom", None),
            P("dom"),
            P("dom"),
            P(),
            P("dom"),
        ),
        out_specs=(P("dom", None), P("dom", "rot", None, None)),
        check_vma=False,
    )
```

profile of v0, /device:TPU:0, one launch (start us, length us, event | category | flops | bytes accessed | tf_op | source)
XLA Modules:
  0.0 107.4 jit_solution(16326860194347295726)
XLA Ops:
  7.2 1.6 %reshape.397 = bf16[16,4096]{1,0:T(8,128)(2,1)} reshape(bf16[4,4,4096]{2,1,0:T(4,128)(2,1)} %param.19) | data formatting | bytes 262144 | tf_op jit(solution)/shard_map/reshape | solution.py:205
  10.1 0.8 select_reduce_fusion.1
  12.9 1.6 %fusion.28 = (s32[1]{0:T(128)}, s32[1]{0:T(128)}, s32[1]{0:T(128)}, s32[1]{0:T(128)}, s32[1]{0:T(128)}, /*index=5*/s32[1]{0:T(128)}, s32[1]{0:T(128)}, s32[1]{0:T(128)}) fusion(s32[8]{0:T(128)} %param.21), kind=kLoop, calls=%fused_computation.98 | loop fusion | bytes 64 | tf_op jit(solution)/shard_map/jit(_take)/gather | solution.py:237
  15.3 4.3 %compare_select_fusion.2 = (s32[512,1]{0,1:T(1,128)S(1)}, s32[512,1]{0,1:T(1,128)S(1)}) fusion(s32[]{:T(128)} %bitcast.15, s32[]{:T(128)} %bitcast.16, s32[]{:T(128)} %bitcast.17, s32[]{:T(128)} %bitcast.18, s32[]{:T(128)} %bitcast.19, s32[]{:T(128)} %bitcast.21, s32[]{:T(128)} %bitcast.20, s32[512,1]{0,1:T(1,128)S(1)} %bitcast.77, s32[512,1]{0,1:T(1,128)S(1)} %bitcast.76), kind=kLoop, calls=%fused_computation.19 | loop fusion | flops 7168 | bytes 8220 | tf_op jit(solution)/shard_map/jit(_take)/gather | solution.py:237
  19.7 4.4 %compare_select_fusion.3 = f32[512,1]{0,1:T(1,128)S(1)} fusion(s32[512,1]{0,1:T(1,128)S(1)} %get-tuple-element.23, f32[]{:T(128)} %bitcast.24, f32[]{:T(128)} %bitcast.25, f32[]{:T(128)} %bitcast.26, f32[]{:T(128)} %bitcast.27, f32[]{:T(128)} %bitcast.28, f32[]{:T(128)} %bitcast.30, f32[]{:T(128)} %bitcast.29), kind=kLoop, calls=%fused_computation.20 | loop fusion | flops 6144 | bytes 4124 | tf_op jit(solution)/shard_map/jit(_take)/gather | solution.py:236
  24.1 1.4 %select_select_fusion = bf16[512]{0:T(512)(128)(2,1)S(1)} fusion(pred[512]{0:T(512)(128)(4,1)S(1)} %compare_reduce_fusion, f32[512]{0:T(512)S(1)} %bitcast.78, bf16[]{:T(256)} %bitcast.23, s32[4,128]{1,0:T(4,128)} %constant.276.clone.1, s32[4]{0:T(128)S(1)} %iota_multiply_fusion), kind=kLoop, calls=%fused_computation.51 | loop fusion | flops 5120 | bytes 5650 | tf_op jit(solution)/shard_map/jit(_take)/select_n | solution.py:236
  25.5 1.4 %add_select_fusion = (s32[512]{0:T(512)S(1)}, s32[512]{0:T(512)S(1)}) fusion(pred[512]{0:T(512)(128)(4,1)S(1)} %compare_reduce_fusion, s32[512]{0:T(512)S(1)} %bitcast.75, s32[]{:T(128)} %bitcast.14, s32[4,128]{1,0:T(4,128)} %constant.276.clone.1, s32[4]{0:T(128)S(1)} %iota_multiply_fusion), kind=kLoop, calls=%fused_computation.42 | loop fusion | flops 8192 | bytes 8724 | tf_op jit(solution)/shard_map/jit(remainder)/select_n | solution.py:239
  26.9 3.5 %convolution_convert_fusion.2 = bf16[256,4096]{1,0:T(8,128)(2,1)S(1)} fusion(bf16[512,4096]{1,0:T(8,128)(2,1)} %bitcast.72, bf16[512]{0:T(512)(128)(2,1)S(1)} %select_select_fusion, s32[512]{0:T(512)S(1)} %get-tuple-element.52, s32[512]{0:T(512)S(1)} %get-tuple-element.51, s32[256]{0:T(256)S(1)} %get-tuple-element.53, s32[256]{0:T(256)S(1)} %get-tuple-element.54), kind=kOutput, calls=%fused_computation.2 | convolution fusion | flops 1075314688 | bytes 6298624 | tf_op jit(solution)/shard_map/dot_general | solution.py:243
  30.5 1.1 slice.87
  32.5 5.7 %convolution_convert_fusion.1 = bf16[384,4096]{1,0:T(8,128)(2,1)} fusion(bf16[384,512]{0,1:T(8,128)(2,1)S(1)} %mul.72, bf16[512,4096]{1,0:T(8,128)(2,1)} %bitcast.73), kind=kOutput, calls=%fused_computation.1 | convolution fusion | flops 1612185600 | bytes 7733248 | tf_op jit(solution)/shard_map/dot_general | solution.py:280
  38.2 1.5 %add_convert_fusion = bf16[128,4096]{1,0:T(8,128)(2,1)S(1)} fusion(bf16[128,4096]{1,0:T(8,128)(2,1)} %collective-permute-done, bf16[256,4096]{1,0:T(8,128)(2,1)S(1)} %convolution_convert_fusion.2), kind=kLoop, calls=%fused_computation.3 | loop fusion | flops 2097152 | bytes 3145728 | tf_op jit(solution)/shard_map/convert_element_type | solution.py:246
  39.7 0.9 fusion.27
  40.7 3.3 %collective-permute-start.1 = (bf16[16,4096]{1,0:T(8,128)(2,1)}, bf16[16,4096]{1,0:T(8,128)(2,1)S(1)}, u32[]{:S(2)}, u32[]{:S(2)}) collective-permute-start(bf16[16,4096]{1,0:T(8,128)(2,1)} %get-tuple-element.32), channel_id=1, source_target_pairs={{0,16},{8,24},{16,0},{24,8},{32,48},{40,56},{48,32},{56,40},{64,80... | collective-permute-start | bytes 393224 | tf_op jit(solution)/shard_map/ppermute | solution.py:254
  43.9 1.9 %collective-permute-start.2 = (bf16[16,4096]{1,0:T(8,128)(2,1)}, bf16[16,4096]{1,0:T(8,128)(2,1)}, u32[]{:S(2)}, u32[]{:S(2)}) collective-permute-start(bf16[16,4096]{1,0:T(8,128)(2,1)} %get-tuple-element.31), channel_id=1, source_target_pairs={{0,32},{8,40},{16,48},{24,56},{32,64},{40,72},{48,80},{56,88},{64,... | collective-permute-start | bytes 393224 | tf_op jit(solution)/shard_map/ppermute | solution.py:254
  46.0 0.9 mul.77
  47.5 1.9 %copy-done = bf16[384,4096]{1,0:T(8,128)(2,1)S(1)} copy-done((bf16[384,4096]{1,0:T(8,128)(2,1)S(1)}, bf16[384,4096]{1,0:T(8,128)(2,1)}, u32[]{:S(2)}) %copy-start) | copy-done | bytes 3145752
  49.5 1.1 %particle_z.1.zp_ref = bf16[4,1536,256]{2,1,0:T(8,128)(2,1)S(1)} custom-call(s32[1]{0:T(128)} %bitcast.4.count_ref, bf16[4,96,4096]{2,1,0:T(8,128)(2,1)S(1)} %bitcast.69, bf16[256,256]{1,0:T(8,128)(2,1)S(1)} %copy-done.3), custom_call_target="tpu_custom_call" | custom-call | tf_op jit(solution)/shard_map/particle_z/pallas_call | solution.py:282
  50.6 2.1 %collective-permute-start.3 = (bf16[16,4096]{1,0:T(8,128)(2,1)S(1)}, bf16[16,4096]{1,0:T(8,128)(2,1)S(1)}, u32[]{:S(2)}, u32[]{:S(2)}) collective-permute-start(bf16[16,4096]{1,0:T(8,128)(2,1)S(1)} %copy-done.12), channel_id=1, source_target_pairs={{0,48},{8,56},{16,32},{24,40},{32,80},{40,88},{48,64},{56,72},{64,... | collective-permute-start | bytes 393224 | tf_op jit(solution)/shard_map/ppermute | solution.py:254
  52.7 2.0 %collective-permute-start.4 = (bf16[16,4096]{1,0:T(8,128)(2,1)S(1)}, bf16[16,4096]{1,0:T(8,128)(2,1)S(1)}, u32[]{:S(2)}, u32[]{:S(2)}) collective-permute-start(bf16[16,4096]{1,0:T(8,128)(2,1)S(1)} %copy-done.11), channel_id=1, source_target_pairs={{0,64},{8,72},{16,80},{24,88},{32,96},{40,104},{48,112},{56,120},{... | collective-permute-start | bytes 393224 | tf_op jit(solution)/shard_map/ppermute | solution.py:254
  54.7 3.9 %collective-permute-start.5 = (bf16[16,4096]{1,0:T(8,128)(2,1)S(1)}, bf16[16,4096]{1,0:T(8,128)(2,1)S(1)}, u32[]{:S(2)}, u32[]{:S(2)}) collective-permute-start(bf16[16,4096]{1,0:T(8,128)(2,1)S(1)} %copy-done.10), channel_id=1, source_target_pairs={{0,80},{8,88},{16,64},{24,72},{32,112},{40,120},{48,96},{56,104},{... | collective-permute-start | bytes 393224 | tf_op jit(solution)/shard_map/ppermute | solution.py:254
  58.5 1.3 %collective-permute-start.6 = (bf16[16,4096]{1,0:T(8,128)(2,1)S(1)}, bf16[16,4096]{1,0:T(8,128)(2,1)S(1)}, u32[]{:S(2)}, u32[]{:S(2)}) collective-permute-start(bf16[16,4096]{1,0:T(8,128)(2,1)S(1)} %copy-done.9), channel_id=1, source_target_pairs={{0,96},{8,104},{16,112},{24,120},{32,0},{40,8},{48,16},{56,24},{64... | collective-permute-start | bytes 393224 | tf_op jit(solution)/shard_map/ppermute | solution.py:254
  59.9 1.3 %collective-permute-start.7 = (bf16[16,4096]{1,0:T(8,128)(2,1)S(1)}, bf16[16,4096]{1,0:T(8,128)(2,1)S(1)}, u32[]{:S(2)}, u32[]{:S(2)}) collective-permute-start(bf16[16,4096]{1,0:T(8,128)(2,1)S(1)} %copy-done.8), channel_id=1, source_target_pairs={{0,112},{8,120},{16,96},{24,104},{32,16},{40,24},{48,0},{56,8},{64... | collective-permute-start | bytes 393224 | tf_op jit(solution)/shard_map/ppermute | solution.py:254
  61.2 5.8 %collective-permute-done.4.refs_4_ = bf16[16,4096]{1,0:T(8,128)(2,1)S(1)} collective-permute-done((bf16[16,4096]{1,0:T(8,128)(2,1)S(1)}, bf16[16,4096]{1,0:T(8,128)(2,1)S(1)}, u32[]{:S(2)}, u32[]{:S(2)}) %collective-permute-start.4) | collective-permute-done | bytes 131104 | tf_op jit(solution)/shard_map/ppermute | solution.py:254
  67.0 1.9 %collective-permute-done.6.refs_6_ = bf16[16,4096]{1,0:T(8,128)(2,1)S(1)} collective-permute-done((bf16[16,4096]{1,0:T(8,128)(2,1)S(1)}, bf16[16,4096]{1,0:T(8,128)(2,1)S(1)}, u32[]{:S(2)}, u32[]{:S(2)}) %collective-permute-start.6) | collective-permute-done | bytes 131104 | tf_op jit(solution)/shard_map/ppermute | solution.py:254
  68.9 2.5 %yz_planes.1 = bf16[1024,128]{1,0:T(8,128)(2,1)S(1)} custom-call(bf16[16,4096]{1,0:T(8,128)(2,1)S(1)} %get-tuple-element.33.refs_0_, bf16[16,4096]{1,0:T(8,128)(2,1)S(1)} %collective-permute-done.1.refs_1_, bf16[16,4096]{1,0:T(8,128)(2,1)} %collective-permute-done.2.refs_2_, bf16[16,4096]{1,0:T(8,128)(2,1)S(1)} %collective-permute-done.3.refs_3_, ...), custom_call_target="tpu_custom_call" | custom-call | tf_op jit(solution)/shard_map/yz_planes/pallas_call | solution.py:258
  72.1 5.9 %all-to-all-start.1 = ((bf16[16,64,128]{2,1,0:T(8,128)(2,1)}), bf16[16,64,128]{2,1,0:T(8,128)(2,1)S(1)}, u32[]{:S(2)}, u32[]{:S(2)}) async-start(bf16[16,64,128]{2,1,0:T(8,128)(2,1)} %bitcast.71), calls=%async_computation.1 | async-start | bytes 524288 | tf_op jit(solution)/shard_map/all_to_all | solution.py:266
  78.0 2.8 %convolution_convert_fusion = bf16[384,4096]{1,0:T(8,128)(2,1)S(1)} fusion(bf16[384,256]{0,1:T(8,128)(2,1)} %mul.77, bf16[256,4096]{1,0:T(8,128)(2,1)} %all-gather.2.cloned.1.call-done), kind=kOutput, calls=%fused_computation | convolution fusion | flops 806879232 | bytes 5439488 | tf_op jit(solution)/shard_map/dot_general | solution.py:301
  81.8 5.8 %all-to-all-done.1.rows_ref = bf16[16,64,128]{2,1,0:T(8,128)(2,1)S(1)} async-done(((bf16[16,64,128]{2,1,0:T(8,128)(2,1)}), bf16[16,64,128]{2,1,0:T(8,128)(2,1)S(1)}, u32[]{:S(2)}, u32[]{:S(2)}) %all-to-all-start.1) | async-done | bytes 262176 | tf_op jit(solution)/shard_map/all_to_all | solution.py:266
  88.2 5.2 %all-to-all-start = ((f32[8,4,512]{2,1,0:T(4,128)}), f32[8,4,512]{2,1,0:T(4,128)S(1)}, u32[]{:S(2)}, u32[]{:S(2)}) async-start(f32[8,4,512]{2,1,0:T(4,128)} %tile.9), calls=%async_computation | async-start | bytes 131072 | tf_op jit(solution)/shard_map/all_to_all | solution.py:334
  93.5 1.0 copy-done.4
  94.5 1.6 %x_rows.1 = f32[4,4,64,128]{3,2,1,0:T(8,128)} custom-call(bf16[16,64,128]{2,1,0:T(8,128)(2,1)S(1)} %all-to-all-done.1.rows_ref, bf16[4,256,256]{2,1,0:T(8,128)(2,1)S(1)} %copy-done.4), custom_call_target="tpu_custom_call" | custom-call | tf_op jit(solution)/shard_map/x_rows/pallas_call | solution.py:267
  96.1 3.7 %all-to-all-done = f32[8,4,512]{2,1,0:T(4,128)S(1)} async-done(((f32[8,4,512]{2,1,0:T(4,128)}), f32[8,4,512]{2,1,0:T(4,128)S(1)}, u32[]{:S(2)}, u32[]{:S(2)}) %all-to-all-start) | async-done | bytes 65568 | tf_op jit(solution)/shard_map/all_to_all | solution.py:334
  (68 shorter events, 8.4 us)
Async XLA Ops:
  7.2 70.9 %all-gather.2.cloned.1.call-start = ((), (), s32[]{:S(2)}) async-start(), calls=%async_computation.2 | async-start | bytes 2228224 | tf_op jit(solution)/shard_map/all_gather | solution.py:204
  26.9 4.6 %copy-start.16 = (s32[8,1]{0,1:T(1,128)S(1)}, s32[8,1]{0,1:T(1,128)}, u32[]{:S(2)}) copy-start(s32[8,1]{0,1:T(1,128)} %param.20) | copy-start | bytes 100
  26.9 4.9 %copy-start.15 = (bf16[96,64]{0,1:T(8,128)(2,1)S(1)}, bf16[96,64]{0,1:T(8,128)(2,1)}, u32[]{:S(2)}) copy-start(bf16[96,64]{0,1:T(8,128)(2,1)} %constant.282.clone) | copy-start | bytes 36868
  30.5 2.0 %copy-start.13 = (s32[8]{0:T(128)S(1)}, s32[8]{0:T(128)}, u32[]{:S(2)}) copy-start(s32[8]{0:T(128)} %param.21) | copy-start | bytes 100
  31.5 6.7 %collective-permute-start = (bf16[128,4096]{1,0:T(8,128)(2,1)}, bf16[128,4096]{1,0:T(8,128)(2,1)}, u32[]{:S(2)}, u32[]{:S(2)}) collective-permute-start(bf16[128,4096]{1,0:T(8,128)(2,1)} %slice.87), channel_id=1, source_target_pairs={{0,8},{8,0},{16,24},{24,16},{32,40},{40,32},{48,56},{56,48},{64,72... | collective-permute-start | bytes 3145736 | tf_op jit(solution)/shard_map/ppermute | solution.py:245
  38.2 7.6 %copy-start.14 = (bf16[96,16,4]{0,2,1:T(4,128)(2,1)S(1)}, bf16[96,16,4]{0,2,1:T(4,128)(2,1)}, u32[]{:S(2)}) copy-start(bf16[96,16,4]{0,2,1:T(4,128)(2,1)} %constant.292) | copy-start | bytes 36868
  38.2 9.3 %copy-start.3 = (bf16[256,256]{1,0:T(8,128)(2,1)S(1)}, bf16[256,256]{1,0:T(8,128)(2,1)}, u32[]{:S(2)}) copy-start(bf16[256,256]{1,0:T(8,128)(2,1)} %constant.283.clone.table_ref) | copy-start | bytes 393220
  40.7 17.9 %collective-permute-start.1 = (bf16[16,4096]{1,0:T(8,128)(2,1)}, bf16[16,4096]{1,0:T(8,128)(2,1)S(1)}, u32[]{:S(2)}, u32[]{:S(2)}) collective-permute-start(bf16[16,4096]{1,0:T(8,128)(2,1)} %get-tuple-element.32), channel_id=1, source_target_pairs={{0,16},{8,24},{16,0},{24,8},{32,48},{40,56},{48,32},{56,40},{64,80... | collective-permute-start | bytes 393224 | tf_op jit(solution)/shard_map/ppermute | solution.py:254
  43.9 15.9 %collective-permute-start.2 = (bf16[16,4096]{1,0:T(8,128)(2,1)}, bf16[16,4096]{1,0:T(8,128)(2,1)}, u32[]{:S(2)}, u32[]{:S(2)}) collective-permute-start(bf16[16,4096]{1,0:T(8,128)(2,1)} %get-tuple-element.31), channel_id=1, source_target_pairs={{0,32},{8,40},{16,48},{24,56},{32,64},{40,72},{48,80},{56,88},{64,... | collective-permute-start | bytes 393224 | tf_op jit(solution)/shard_map/ppermute | solution.py:254
  47.5 1.9 %copy-start = (bf16[384,4096]{1,0:T(8,128)(2,1)S(1)}, bf16[384,4096]{1,0:T(8,128)(2,1)}, u32[]{:S(2)}) copy-start(bf16[384,4096]{1,0:T(8,128)(2,1)} %convolution_convert_fusion.1) | copy-start | bytes 9437188
  49.4 1.2 %copy-start.12 = (bf16[16,4096]{1,0:T(8,128)(2,1)S(1)}, bf16[16,4096]{1,0:T(8,128)(2,1)}, u32[]{:S(2)}) copy-start(bf16[16,4096]{1,0:T(8,128)(2,1)} %get-tuple-element.30) | copy-start | bytes 393220
  49.4 3.3 %copy-start.11 = (bf16[16,4096]{1,0:T(8,128)(2,1)S(1)}, bf16[16,4096]{1,0:T(8,128)(2,1)}, u32[]{:S(2)}) copy-start(bf16[16,4096]{1,0:T(8,128)(2,1)} %get-tuple-element.29) | copy-start | bytes 393220
  49.4 5.2 %copy-start.10 = (bf16[16,4096]{1,0:T(8,128)(2,1)S(1)}, bf16[16,4096]{1,0:T(8,128)(2,1)}, u32[]{:S(2)}) copy-start(bf16[16,4096]{1,0:T(8,128)(2,1)} %get-tuple-element.28) | copy-start | bytes 393220
  49.4 9.1 %copy-start.9 = (bf16[16,4096]{1,0:T(8,128)(2,1)S(1)}, bf16[16,4096]{1,0:T(8,128)(2,1)}, u32[]{:S(2)}) copy-start(bf16[16,4096]{1,0:T(8,128)(2,1)} %get-tuple-element.27) | copy-start | bytes 393220
  49.5 10.4 %copy-start.8 = (bf16[16,4096]{1,0:T(8,128)(2,1)S(1)}, bf16[16,4096]{1,0:T(8,128)(2,1)}, u32[]{:S(2)}) copy-start(bf16[16,4096]{1,0:T(8,128)(2,1)} %get-tuple-element.26) | copy-start | bytes 393220
  49.5 19.4 %copy-start.1 = (bf16[2048,1024]{1,0:T(8,128)(2,1)S(1)}, bf16[2048,1024]{1,0:T(8,128)(2,1)}, u32[]{:S(2)}) copy-start(bf16[2048,1024]{1,0:T(8,128)(2,1)} %constant.280.clone.refs_9_) | copy-start | bytes 12582916
  49.5 19.4 %copy-start.6 = (bf16[128,256]{1,0:T(8,128)(2,1)S(1)}, bf16[128,256]{1,0:T(8,128)(2,1)}, u32[]{:S(2)}) copy-start(bf16[128,256]{1,0:T(8,128)(2,1)} %constant.293.refs_8_) | copy-start | bytes 196612
  50.6 10.6 %collective-permute-start.3 = (bf16[16,4096]{1,0:T(8,128)(2,1)S(1)}, bf16[16,4096]{1,0:T(8,128)(2,1)S(1)}, u32[]{:S(2)}, u32[]{:S(2)}) collective-permute-start(bf16[16,4096]{1,0:T(8,128)(2,1)S(1)} %copy-done.12), channel_id=1, source_target_pairs={{0,48},{8,56},{16,32},{24,40},{32,80},{40,88},{48,64},{56,72},{64,... | collective-permute-start | bytes 393224 | tf_op jit(solution)/shard_map/ppermute | solution.py:254
  52.7 14.3 %collective-permute-start.4 = (bf16[16,4096]{1,0:T(8,128)(2,1)S(1)}, bf16[16,4096]{1,0:T(8,128)(2,1)S(1)}, u32[]{:S(2)}, u32[]{:S(2)}) collective-permute-start(bf16[16,4096]{1,0:T(8,128)(2,1)S(1)} %copy-done.11), channel_id=1, source_target_pairs={{0,64},{8,72},{16,80},{24,88},{32,96},{40,104},{48,112},{56,120},{... | collective-permute-start | bytes 393224 | tf_op jit(solution)/shard_map/ppermute | solution.py:254
  54.7 12.3 %collective-permute-start.5 = (bf16[16,4096]{1,0:T(8,128)(2,1)S(1)}, bf16[16,4096]{1,0:T(8,128)(2,1)S(1)}, u32[]{:S(2)}, u32[]{:S(2)}) collective-permute-start(bf16[16,4096]{1,0:T(8,128)(2,1)S(1)} %copy-done.10), channel_id=1, source_target_pairs={{0,80},{8,88},{16,64},{24,72},{32,112},{40,120},{48,96},{56,104},{... | collective-permute-start | bytes 393224 | tf_op jit(solution)/shard_map/ppermute | solution.py:254
  58.5 10.4 %collective-permute-start.6 = (bf16[16,4096]{1,0:T(8,128)(2,1)S(1)}, bf16[16,4096]{1,0:T(8,128)(2,1)S(1)}, u32[]{:S(2)}, u32[]{:S(2)}) collective-permute-start(bf16[16,4096]{1,0:T(8,128)(2,1)S(1)} %copy-done.9), channel_id=1, source_target_pairs={{0,96},{8,104},{16,112},{24,120},{32,0},{40,8},{48,16},{56,24},{64... | collective-permute-start | bytes 393224 | tf_op jit(solution)/shard_map/ppermute | solution.py:254
  59.9 9.0 %collective-permute-start.7 = (bf16[16,4096]{1,0:T(8,128)(2,1)S(1)}, bf16[16,4096]{1,0:T(8,128)(2,1)S(1)}, u32[]{:S(2)}, u32[]{:S(2)}) collective-permute-start(bf16[16,4096]{1,0:T(8,128)(2,1)S(1)} %copy-done.8), channel_id=1, source_target_pairs={{0,112},{8,120},{16,96},{24,104},{32,16},{40,24},{48,0},{56,8},{64... | collective-permute-start | bytes 393224 | tf_op jit(solution)/shard_map/ppermute | solution.py:254
  71.4 0.7 copy-start.2
  72.1 8.7 %copy-start.7 = (bf16[16,40]{1,0:T(8,128)(2,1)S(1)}, bf16[16,40]{1,0:T(8,128)(2,1)}, u32[]{:S(2)}) copy-start(bf16[16,40]{1,0:T(8,128)(2,1)} %constant.284.clone.ex_ref) | copy-start | bytes 3844
  72.1 15.4 %all-to-all-start.1 = ((bf16[16,64,128]{2,1,0:T(8,128)(2,1)}), bf16[16,64,128]{2,1,0:T(8,128)(2,1)S(1)}, u32[]{:S(2)}, u32[]{:S(2)}) async-start(bf16[16,64,128]{2,1,0:T(8,128)(2,1)} %bitcast.71), calls=%async_computation.1 | async-start | bytes 524288 | tf_op jit(solution)/shard_map/all_to_all | solution.py:266
  78.0 2.8 %copy-start.5 = (bf16[512,128]{1,0:T(8,128)(2,1)S(1)}, bf16[512,128]{1,0:T(8,128)(2,1)}, u32[]{:S(2)}) copy-start(bf16[512,128]{1,0:T(8,128)(2,1)} %constant.285.clone.wz_ref) | copy-start | bytes 393220
  88.2 11.6 %all-to-all-start = ((f32[8,4,512]{2,1,0:T(4,128)}), f32[8,4,512]{2,1,0:T(4,128)S(1)}, u32[]{:S(2)}, u32[]{:S(2)}) async-start(f32[8,4,512]{2,1,0:T(4,128)} %tile.9), calls=%async_computation | async-start | bytes 131072 | tf_op jit(solution)/shard_map/all_to_all | solution.py:334
  93.5 1.0 copy-start.4
Sparse Core Ops, SparseCore 0:
  10.5 58.2 all-gather.1
where the time goes:
time: 109 us; the launch traced here: 107 us
  starting transfers between devices  26.8 us (25%)
  other arithmetic  18.2 us (17%)
  waiting for transfers between devices  17.2 us (16%)
  between operations  15 us (14%)
  local copies, waits for them, and re-layouts  12.2 us (11%)
  matrix products  12 us (11%)
  Pallas kernels  5.93 us (5%)
    ppermute x7, starting transfers between devices, shards(): lax.ppermute(pair_sum[k * per_chip:(k + 1) * per_chip], 'dom', route)  15.7 us
    ppermute x7, waiting for transfers between devices, shards(): lax.ppermute(pair_sum[k * per_chip:(k + 1) * per_chip], 'dom', route)  7.71 us
    all_to_all x1, starting transfers between devices, shards(): by_rows = lax.all_to_all(grids, 'dom', 0, 0, tiled=True)  5.87 us
    all_to_all x1, waiting for transfers between devices, shards(): by_rows = lax.all_to_all(grids, 'dom', 0, 0, tiled=True)  5.79 us
    dot_general x1, matrix products, shards(): along_x = jnp.dot(pick, flat, preferred_element_type=F32).astype(BF)  5.68 us
    all_to_all x1, starting transfers between devices, shards(): lax.all_to_all(jnp.tile(slot_scores, (8, 1)), 'rot', 0, 0, tiled=True)  5.22 us
    gather x1, other arithmetic, shards(): col_weight = jnp.repeat(weight, BOX, total_repeat_length=block_size * BOX)  4.44 us
    gather x2, other arithmetic, shards(): col_rot = jnp.repeat(part_rot, BOX, total_repeat_length=block_size * BOX)  4.33 us
  transfers between devices with their start and end apart: 11, of which 4 were waited for; matrix products, arithmetic and copies ran while one was open for 33% of the time, Pallas kernels for 6%

commit v1 on v0

--- a/solution.py
+++ b/solution.py
@@ -17,6 +17,8 @@
 KXV = 40
 PAIRS = BOX // 2
 DOM = 16
+CHIPS = DOM // 2
+SAME_CORE = [[2 * chip + core for chip in range(CHIPS)] for core in range(2)]
 BF = jnp.bfloat16
 F32 = jnp.float32
 
@@ -89,27 +91,54 @@
 
 
 STEP = 8
-
-
-def particle_kernel(count_ref, xp_ref, table_ref, out_ref):
-    @pl.when(pl.program_id(0) < count_ref[0])
+CHUNK = 4
+
+
+def front_kernel(own_ref, pick_ref, flat_ref, table_ref, own_out, spectra_out):
+    flat = flat_ref[...]
+    own_out[...] = jnp.dot(own_ref[...], flat, preferred_element_type=F32).astype(BF)
+    along_x = jnp.dot(pick_ref[...], flat, preferred_element_type=F32).astype(BF)
+    table = table_ref[...]
+    for slot in range(CAP):
+        part = z_stage(along_x[slot * 2 * KXP : (slot + 1) * 2 * KXP], table, 0, CHUNK)
+        spectra_out[slot] = part.astype(BF)
+
+
+def score_kernel(
+    count_ref,
+    zp_ref,
+    pick_own_ref,
+    pick_other_ref,
+    own_ref,
+    other_ref,
+    table_ref,
+    ex_ref,
+    wz_ref,
+    out_ref,
+    x_s,
+    p_s,
+    r_s,
+    o_s,
+    a_s,
+):
+    slot = pl.program_id(0)
+
+    @pl.when((slot == 0) & (count_ref[0] > 0))
+    def _():
+        for start in range(0, BOX * BOX, 512):
+            lanes = slice(start, start + 512)
+            part = jnp.dot(pick_own_ref[...], own_ref[:, lanes], preferred_element_type=F32)
+            part = part + jnp.dot(
+                pick_other_ref[...], other_ref[:, lanes], preferred_element_type=F32
+            )
+            x_s[:, :, lanes] = part.astype(BF).reshape(CAP, 2 * KXP, 512)
+
+    @pl.when(slot < count_ref[0])
     def _():
         table = table_ref[...]
+        xr = x_s.at[slot]
         for start in range(0, PAIRS, STEP):
-            part = z_stage(xp_ref, table, start, STEP)
-            out_ref[start * KXP : (start + STEP) * KXP, :] = part.astype(BF)
-
-    @pl.when(pl.program_id(0) >= count_ref[0])
-    def _():
-        out_ref[...] = jnp.zeros_like(out_ref)
-
-
-def score_kernel(count_ref, zp_ref, xr_ref, table_ref, ex_ref, wz_ref, out_ref, p_s, r_s, o_s, a_s):
-    @pl.when(pl.program_id(0) < count_ref[0])
-    def _():
-        table = table_ref[...]
-        for start in range(0, PAIRS, STEP):
-            part = z_stage(xr_ref, table, start, STEP)
+            part = z_stage(xr, table, start, STEP)
             part = part.astype(BF).astype(F32).reshape(STEP, KXP, 4 * BOX)
             r_s[start : start + STEP] = part[:, :KXV, :]
             mine = zp_ref[start * KXP : (start + STEP) * KXP, :].astype(F32)
@@ -153,16 +182,16 @@
         final = jnp.dot(both, wz_ref[...], preferred_element_type=F32)
         out_ref[...] = final * (float(BOX) ** -3.5)
 
-    @pl.when(pl.program_id(0) >= count_ref[0])
+    @pl.when(slot >= count_ref[0])
     def _():
         out_ref[...] = jnp.zeros_like(out_ref)
 
 
-def yz_kernel(*refs):
-    own_ref, part_refs, (z_ref, y_ref, out_ref) = refs[0], refs[1:8], refs[8:]
-    total = own_ref[...].astype(F32)
-    for part in part_refs:
-        total = total + part[...].astype(F32)
+def yz_kernel(parts_ref, z_ref, y_ref, out_ref):
+    rows = parts_ref.shape[0] // CHIPS
+    total = parts_ref[0:rows].astype(F32)
+    for chip in range(1, CHIPS):
+        total = total + parts_ref[chip * rows : (chip + 1) * rows].astype(F32)
     total = total.astype(BF)
     stacked = jnp.concatenate([total[:, 128 * j : 128 * (j + 1)] for j in range(PAIRS)], axis=0)
     z_part = jnp.dot(stacked, z_ref[...], preferred_element_type=F32).astype(BF)
@@ -197,13 +226,17 @@
     block_size = particles.shape[0]
     planes = references.shape[1]
     voxels = BOX * BOX
-    dom = lax.axis_index("dom")
+    per_chip = ROT_CLS * planes
+    columns = block_size * BOX
+    core = lax.axis_index("dom") % 2
     owner = lax.axis_index("rot")
-    chip, core = dom // 2, dom % 2
-
-    all_refs = lax.all_gather(
-        references.reshape(ROT_CLS * planes, voxels), "dom", axis=0, tiled=True
+    to_other = [(i, i ^ 1) for i in range(DOM)]
+
+    mine_refs = references.reshape(per_chip, voxels)
+    refs_own = lax.all_to_all(
+        jnp.tile(mine_refs, (CHIPS, 1)), "dom", 0, 0, tiled=True, axis_index_groups=SAME_CORE
     )
+    refs_other = lax.ppermute(refs_own, "dom", to_other)
 
     rows_all = jnp.arange(block_size, dtype=jnp.int32)
     classes = part_class[:, 0]
@@ -217,89 +250,74 @@
         bucket[:, None] == bucket_ids[None, :], bucket_weights[None, :].astype(F32), 0.0
     )
     weight = jnp.where(mine, jnp.sum(level, axis=1), 0.0)
+    slot_of = jnp.where(mine, rank, -1)
+
+    col = np.arange(columns)
+    col_is = jnp.asarray(col[None, :] // BOX == np.arange(block_size)[:, None])
+    col_weight = jnp.sum(jnp.where(col_is, weight[:, None], 0.0), axis=0)
+    col_rot = jnp.sum(jnp.where(col_is, part_rot[:, None], 0), axis=0)
+    col_slot = jnp.sum(jnp.where(col_is, slot_of[:, None], 0), axis=0)
+
+    flat = particles.reshape(columns, voxels)
+    row = np.arange(CHIPS * per_chip)
+    row_chip, row_r, row_x = row // per_chip, (row // planes) % ROT_CLS, row % planes
+    row_r = jnp.asarray(row_r.astype(np.int32))
+
+    def spread(to_core):
+        want_x = jnp.asarray((row_chip * 2 * planes + row_x).astype(np.int32)) + to_core * planes
+        hit = want_x[:, None] == jnp.asarray((col % BOX).astype(np.int32))[None, :]
+        return jnp.where(hit & (row_r[:, None] == col_rot[None, :]), col_weight[None, :], 0.0).astype(BF)
+
+    to_send = jnp.dot(spread(1 - core), flat, preferred_element_type=F32).astype(BF)
+    other = lax.ppermute(to_send, "dom", to_other)
+
+    x_half = x_half_table()
+    slot_rows = np.arange(CAP * 2 * KXP) // (2 * KXP)
+    slot_rows = jnp.asarray(slot_rows.astype(np.int32))
+    pick = jnp.where(
+        slot_rows[:, None] == col_slot[None, :],
+        jnp.asarray(np.tile(x_half, (CAP, block_size)).astype(BF)),
+        jnp.zeros((), BF),
+    )
+    z_table = jnp.asarray(z_complex_table().astype(BF))
+    own, spectra = pl.pallas_call(
+        front_kernel,
+        out_shape=(
+            jax.ShapeDtypeStruct((CHIPS * per_chip, voxels), BF),
+            jax.ShapeDtypeStruct((CAP, PAIRS * KXP, 4 * BOX), BF),
+        ),
+        grid=(PAIRS // CHUNK,),
+        in_specs=[
+            pl.BlockSpec((CHIPS * per_chip, columns), lambda i: (0, 0)),
+            pl.BlockSpec((CAP * 2 * KXP, columns), lambda i: (0, 0)),
+            pl.BlockSpec((columns, 128 * CHUNK), lambda i: (0, i)),
+            pl.BlockSpec((4 * BOX, 4 * BOX), lambda i: (0, 0)),
+        ],
+        out_specs=(
+            pl.BlockSpec((CHIPS * per_chip, 128 * CHUNK), lambda i: (0, i)),
+            pl.BlockSpec((CAP, CHUNK * KXP, 4 * BOX), lambda i: (0, i, 0)),
+        ),
+        compiler_params=PARAMS,
+        name="front",
+    )(spread(core), pick, flat, z_table)
+    pair_sum = (own.astype(F32) + other.astype(F32)).astype(BF)
+    arrived = lax.all_to_all(pair_sum, "dom", 0, 0, tiled=True, axis_index_groups=SAME_CORE)
+
     slot_ids = jnp.arange(CAP, dtype=jnp.int32)
-    picked = (rank[None, :] == slot_ids[:, None]) & mine[None, :]
-    slot_rot = jnp.sum(jnp.where(picked, part_rot[None, :], 0), axis=1)
-
-    flat = particles.reshape(block_size * BOX, voxels)
-
-    row = jnp.arange(DOM * ROT_CLS * planes, dtype=jnp.int32)
-    row_x = row % planes
-    row_r = (row // planes) % ROT_CLS
-    row_chip = (row // (planes * ROT_CLS)) % 8
-    row_core = row // (planes * ROT_CLS * 8)
-    to_z = (chip // 2 + row_chip // 2) % 4
-    to_y = (chip % 2) ^ (row_chip % 2)
-    to_dom = (to_z * 2 + to_y) * 2 + (core ^ row_core)
-    want_x = to_dom * planes + row_x
-    col = jnp.arange(block_size * BOX, dtype=jnp.int32)
-    col_weight = jnp.repeat(weight, BOX, total_repeat_length=block_size * BOX)
-    col_rot = jnp.repeat(part_rot, BOX, total_repeat_length=block_size * BOX)
-    spread = jnp.where(
-        (want_x[:, None] == (col % BOX)[None, :]) & (row_r[:, None] == col_rot[None, :]),
-        col_weight[None, :],
-        0.0,
-    ).astype(BF)
-    to_send = jnp.dot(spread, flat, preferred_element_type=F32).astype(BF)
-    half_rows = to_send.shape[0] // 2
-    other = lax.ppermute(to_send[half_rows:], "dom", [(i, i ^ 1) for i in range(DOM)])
-    pair_sum = (to_send[:half_rows].astype(F32) + other.astype(F32)).astype(BF)
-    per_chip = ROT_CLS * planes
-    arrived = []
-    for k in range(1, 8):
-        route = []
-        for i in range(DOM):
-            z, y, c = i // 4, (i // 2) % 2, i % 2
-            route.append((i, ((z + k // 2) % 4) * 4 + (y ^ (k % 2)) * 2 + c))
-        arrived.append(lax.ppermute(pair_sum[k * per_chip : (k + 1) * per_chip], "dom", route))
-
-    z_real = jnp.asarray(z_real_table(), F32).astype(BF)
-    y_full = jnp.asarray(y_table(per_chip).astype(BF))
-    grids = pl.pallas_call(
-        yz_kernel,
-        out_shape=jax.ShapeDtypeStruct((BOX * per_chip, 2 * BOX), BF),
-        in_specs=[VMEM] * 10,
-        out_specs=VMEM,
-        compiler_params=PARAMS,
-        name="yz_planes",
-    )(pair_sum[:per_chip], *arrived, z_real, y_full)
-    by_rows = lax.all_to_all(grids, "dom", 0, 0, tiled=True)
-    sums = pl.pallas_call(
-        x_rows_kernel,
-        out_shape=jax.ShapeDtypeStruct((BOX // DOM, ROT_CLS, BOX, 2 * BOX), F32),
-        in_specs=[VMEM] * 2,
-        out_specs=VMEM,
-        compiler_params=PARAMS,
-        name="x_rows",
-    )(by_rows.reshape(DOM, BOX // DOM * per_chip, 2 * BOX), jnp.asarray(x_rows_table()))
-
-    x_half = jnp.asarray(x_half_table().astype(BF))
-    pick = (
-        picked.astype(BF)[:, None, :, None] * x_half[None, :, None, :]
-    ).reshape(CAP * 2 * KXP, block_size * BOX)
-    along_x = jnp.dot(pick, flat, preferred_element_type=F32).astype(BF)
-    z_table = jnp.asarray(z_complex_table().astype(BF))
-    spectra = pl.pallas_call(
-        particle_kernel,
-        out_shape=jax.ShapeDtypeStruct((CAP, PAIRS * KXP, 4 * BOX), BF),
-        grid=(CAP,),
-        in_specs=[
-            SMEM,
-            pl.BlockSpec((None, 2 * KXP, voxels), lambda s: (s, 0, 0)),
-            pl.BlockSpec((4 * BOX, 4 * BOX), lambda s: (0, 0)),
-        ],
-        out_specs=pl.BlockSpec((None, PAIRS * KXP, 4 * BOX), lambda s: (s, 0, 0)),
-        compiler_params=PARAMS,
-        name="particle_z",
-    )(count, along_x.reshape(CAP, 2 * KXP, voxels), z_table)
-
-    rot_ids = jnp.arange(ROT_CLS, dtype=jnp.int32)
-    choose = (slot_rot[:, None] == rot_ids[None, :]).astype(BF)
-    pick_ref = (
-        choose[:, None, None, :, None] * x_half.reshape(1, 2 * KXP, DOM, 1, planes)
-    ).reshape(CAP * 2 * KXP, DOM * per_chip)
-    ref_x = jnp.dot(pick_ref, all_refs, preferred_element_type=F32).astype(BF)
+    slot_rot = jnp.sum(jnp.where(slot_of[None, :] == slot_ids[:, None], part_rot[None, :], 0), axis=1)
+    row_rot = jnp.sum(jnp.where(slot_rows[:, None] == slot_ids[None, :], slot_rot[None, :], 0), axis=1)
+    by_core = x_half.reshape(2 * KXP, CHIPS, 2, 1, planes)
+    by_core = np.broadcast_to(by_core, (2 * KXP, CHIPS, 2, ROT_CLS, planes))
+    by_core = by_core.transpose(2, 0, 1, 3, 4).reshape(2, 2 * KXP, CHIPS * per_chip)
+    by_core = jnp.asarray(np.tile(by_core, (1, CAP, 1)).astype(BF))
+    right = row_rot[:, None] == row_r[None, :]
+    pick_own = jnp.where(right, jnp.where(core == 0, by_core[0], by_core[1]), jnp.zeros((), BF))
+    pick_other = jnp.where(right, jnp.where(core == 0, by_core[1], by_core[0]), jnp.zeros((), BF))
     ex, wz = shift_tables()
+
+    def whole(*shape):
+        return pl.BlockSpec(shape, lambda s: (0,) * len(shape))
+
     slots = pl.pallas_call(
         score_kernel,
         out_shape=jax.ShapeDtypeStruct((CAP, SHIFTS * SHIFTS, 128), F32),
@@ -307,13 +325,17 @@
         in_specs=[
             SMEM,
             pl.BlockSpec((None, PAIRS * KXP, 4 * BOX), lambda s: (s, 0, 0)),
-            pl.BlockSpec((None, 2 * KXP, voxels), lambda s: (s, 0, 0)),
-            pl.BlockSpec((4 * BOX, 4 * BOX), lambda s: (0, 0)),
-            pl.BlockSpec((2 * SHIFTS, KXV), lambda s: (0, 0)),
-            pl.BlockSpec((8 * BOX, 128), lambda s: (0, 0)),
+            whole(CAP * 2 * KXP, CHIPS * per_chip),
+            whole(CAP * 2 * KXP, CHIPS * per_chip),
+            whole(CHIPS * per_chip, voxels),
+            whole(CHIPS * per_chip, voxels),
+            whole(4 * BOX, 4 * BOX),
+            whole(2 * SHIFTS, KXV),
+            whole(8 * BOX, 128),
         ],
         out_specs=pl.BlockSpec((None, SHIFTS * SHIFTS, 128), lambda s: (s, 0, 0)),
         scratch_shapes=[
+            pltpu.VMEM((CAP, 2 * KXP, voxels), BF),
             pltpu.VMEM((PAIRS, KXV, 4 * BOX), F32),
             pltpu.VMEM((PAIRS, KXV, 4 * BOX), F32),
             pltpu.VMEM((PAIRS, KXV, 4 * BOX), F32),
@@ -324,19 +346,40 @@
     )(
         count,
         spectra,
-        ref_x.reshape(CAP, 2 * KXP, voxels),
+        pick_own,
+        pick_other,
+        refs_own,
+        refs_other,
         z_table,
         jnp.asarray(ex.astype(BF)),
         jnp.asarray(wz.astype(BF)),
     )
     slot_scores = slots[:, :, :SHIFTS].reshape(CAP, SHIFTS, SHIFTS, SHIFTS)
     slot_scores = slot_scores.transpose(0, 2, 1, 3).reshape(CAP, SHIFTS**3)
-    everywhere = lax.all_to_all(
-        jnp.tile(slot_scores, (8, 1)), "rot", 0, 0, tiled=True
-    )
+    everywhere = lax.all_to_all(jnp.tile(slot_scores, (8, 1)), "rot", 0, 0, tiled=True)
     place = classes * CAP + rank
     found = (place[:, None] == jnp.arange(8 * CAP, dtype=jnp.int32)[None, :]) & alive[:, None]
     scores = jnp.sum(jnp.where(found[:, :, None], everywhere[None, :, :], 0.0), axis=1)
+
+    z_real = jnp.asarray(z_real_table().astype(BF))
+    y_full = jnp.asarray(y_table(per_chip).astype(BF))
+    grids = pl.pallas_call(
+        yz_kernel,
+        out_shape=jax.ShapeDtypeStruct((BOX * per_chip, 2 * BOX), BF),
+        in_specs=[VMEM] * 3,
+        out_specs=VMEM,
+        compiler_params=PARAMS,
+        name="yz_planes",
+    )(arrived, z_real, y_full)
+    by_rows = lax.all_to_all(grids, "dom", 0, 0, tiled=True)
+    sums = pl.pallas_call(
+        x_rows_kernel,
+        out_shape=jax.ShapeDtypeStruct((BOX // DOM, ROT_CLS, BOX, 2 * BOX), F32),
+        in_specs=[VMEM] * 2,
+        out_specs=VMEM,
+        compiler_params=PARAMS,
+        name="x_rows",
+    )(by_rows.reshape(DOM, BOX // DOM * per_chip, 2 * BOX), jnp.asarray(x_rows_table()))
     return (scores, sums)
 
 

time: 109 us -> 90.4 us (0.83)
  the two profiles are of different devices: /device:TPU:0 before, /device:TPU:1 now
where the time goes in v1:
time: 90.4 us; the launch traced here: 89.7 us
  waiting for transfers between devices  24.2 us (27%)
  starting transfers between devices  23.7 us (26%)
  Pallas kernels  14.4 us (16%)
  other arithmetic  11.9 us (13%)
  local copies, waits for them, and re-layouts  9.9 us (11%)
  matrix products  4.01 us (4%)
  between operations  1.58 us (2%)
    all_to_all x1, waiting for transfers between devices, shards(): lax.all_to_all(pair_sum, 'dom', 0, 0, tiled=True, axis_index_groups=SAME_...  8.32 us
    unnamed x34, local copies, waits for them, and re-layouts  7.95 us
    all_to_all x1, waiting for transfers between devices, shards(): by_rows = lax.all_to_all(grids, 'dom', 0, 0, tiled=True)  7.88 us
    all_to_all x1, starting transfers between devices, shards(): lax.all_to_all(jnp.tile(mine_refs, (CHIPS, 1)), 'dom', 0, 0, tiled=True,...  7.75 us
    all_to_all x1, waiting for transfers between devices, shards(): lax.all_to_all(jnp.tile(mine_refs, (CHIPS, 1)), 'dom', 0, 0, tiled=True,...  7.31 us
    all_to_all x1, starting transfers between devices, shards(): by_rows = lax.all_to_all(grids, 'dom', 0, 0, tiled=True)  5.57 us
    pallas_call x1, Pallas kernels, shards(): pl.pallas_call(front_kernel, out_shape=(jax.ShapeDtypeStruct((CHIPS * per...  5.56 us
    pallas_call x1, Pallas kernels, shards(): pl.pallas_call(score_kernel, out_shape=jax.ShapeDtypeStruct((CAP, SHIFTS...  4.95 us
  transfers between devices with their start and end apart: 6, of which 4 were waited for; matrix products, arithmetic and copies ran while one was open for 8% of the time, Pallas kernels for 14%

profile of v1, /device:TPU:1, one launch (start us, length us, event | category | flops | bytes accessed | tf_op | source)
XLA Modules:
  0.0 89.7 jit_solution(4285665218379743483)
XLA Ops:
  1.4 0.7 convert_element_type.30
  2.0 0.9 %convert_reduce_fusion = s32[8]{0:T(128)S(1)} fusion(s32[8]{0:T(128)} %bitcast.53, pred[8]{0:T(512)(128)(4,1)S(1)} %iota_compare_fusion.5), kind=kLoop, calls=%fused_computation.26 | loop fusion | flops 376 | bytes 72 | tf_op jit(solution)/shard_map/reduce_sum | solution.py:245
  2.9 0.8 select_reduce_fusion.5
  3.8 1.2 %fusion.9 = (s32[8]{0:T(128)}, s32[8]{0:T(128)S(1)}) fusion(s32[8]{0:T(128)S(1)} %convert_reduce_fusion, s32[8,1]{0,1:T(1,128)} %param.24, s32[]{:T(128)} %bitcast.44, s32[]{:T(128)S(6)} %axis_index.22), kind=kLoop, calls=%fused_computation.38 | loop fusion | flops 48 | bytes 136 | tf_op jit(solution)/shard_map/add | solution.py:360
  5.0 0.7 fusion.8
  5.6 0.8 select_reduce_fusion.2
  6.4 0.8 select_reduce_fusion.1
  7.2 0.7 broadcast_add_fusion
  7.8 4.0 %convolution_convert_fusion = bf16[128,4096]{1,0:T(8,128)(2,1)} fusion(bf16[512,4096]{1,0:T(8,128)(2,1)} %bitcast.46, bf16[512]{0:T(512)(128)(2,1)S(1)} %select_reduce_fusion.2, s32[512]{0:T(512)S(1)} %get-tuple-element.7, s32[512]{0:T(512)} %constant.62.clone, s32[128]{0:T(128)S(1)} %get-tuple-element.12, s32[128]{0:T(128)} %constant.60.clone), kind=kOutput, calls=%fused_computation | convolution fusion | flops 537657344 | bytes 5249024 | tf_op jit(solution)/shard_map/dot_general | solution.py:271
  11.9 1.4 %collective-permute-start.1 = (bf16[128,4096]{1,0:T(8,128)(2,1)}, bf16[128,4096]{1,0:T(8,128)(2,1)}, u32[]{:S(2)}, u32[]{:S(2)}) collective-permute-start(bf16[128,4096]{1,0:T(8,128)(2,1)} %convolution_convert_fusion), channel_id=1, source_target_pairs={{0,8},{8,0},{16,24},{24,16},{32,40},{40,32},{48,56},{56,48},{64,72... | collective-permute-start | bytes 3145736 | tf_op jit(solution)/shard_map/ppermute | solution.py:272
  13.3 1.1 %tile.17 = bf16[8,16,4096]{2,1,0:T(8,128)(2,1)} broadcast(bf16[16,4096]{1,0:T(8,128)(2,1)S(1)} %tile.16), dimensions={1,2} | broadcast | bytes 1179648 | tf_op jit(solution)/shard_map/tile | solution.py:237
  14.4 7.8 %all-to-all-start = ((bf16[8,16,4096]{2,1,0:T(8,128)(2,1)}), bf16[8,16,4096]{2,1,0:T(8,128)(2,1)S(1)}, u32[]{:S(2)}, u32[]{:S(2)}) async-start(bf16[8,16,4096]{2,1,0:T(8,128)(2,1)} %tile.17), calls=%async_computation | async-start | bytes 2097152 | tf_op jit(solution)/shard_map/all_to_all | solution.py:236
  22.5 2.2 %copy-done = bf16[8,64,4096]{2,1,0:T(8,128)(2,1)S(1)} copy-done((bf16[8,64,4096]{2,1,0:T(8,128)(2,1)S(1)}, bf16[8,64,4096]{2,1,0:T(8,128)(2,1)}, u32[]{:S(2)}) %copy-start) | copy-done | bytes 4194328
  24.7 5.6 %front.1 = (bf16[128,4096]{1,0:T(8,128)(2,1)S(1)}, bf16[4,1536,256]{2,1,0:T(8,128)(2,1)S(1)}) custom-call(bf16[128,512]{1,0:T(8,128)(2,1)S(1)} %select_convert_fusion.1.own_ref, bf16[384,512]{1,0:T(8,128)(2,1)S(1)} %compare_select_fusion.pick_ref, bf16[512,4096]{1,0:T(8,128)(2,1)S(1)} %bitcast.47, bf16[256,256]{1,0:T(8,128)(2,1)S(1)} %copy-done.5), custom_call_target="tpu_custom_call" | custom-call | tf_op jit(solution)/shard_map/front/pallas_call | solution.py:283
  30.3 1.6 %copy-done.2 = bf16[4,1536,256]{2,1,0:T(8,128)(2,1)} copy-done((bf16[4,1536,256]{2,1,0:T(8,128)(2,1)}, bf16[4,1536,256]{2,1,0:T(8,128)(2,1)S(1)}, u32[]{:S(2)}) %copy-start.2) | copy-done | bytes 3145752
  31.9 7.3 %all-to-all-done = bf16[8,16,4096]{2,1,0:T(8,128)(2,1)S(1)} async-done(((bf16[8,16,4096]{2,1,0:T(8,128)(2,1)}), bf16[8,16,4096]{2,1,0:T(8,128)(2,1)S(1)}, u32[]{:S(2)}, u32[]{:S(2)}) %all-to-all-start) | async-done | bytes 1048608 | tf_op jit(solution)/shard_map/all_to_all | solution.py:236
  39.2 1.1 %collective-permute-start = (bf16[128,4096]{1,0:T(8,128)(2,1)S(1)}, bf16[128,4096]{1,0:T(8,128)(2,1)S(1)}, u32[]{:S(2)}, u32[]{:S(2)}) collective-permute-start(bf16[128,4096]{1,0:T(8,128)(2,1)S(1)} %bitcast.48), channel_id=1, source_target_pairs={{0,8},{8,0},{16,24},{24,16},{32,40},{40,32},{48,56},{56,48},{64,72... | collective-permute-start | bytes 3145736 | tf_op jit(solution)/shard_map/ppermute | solution.py:239
  40.4 2.4 %add_convert_fusion = bf16[128,4096]{1,0:T(8,128)(2,1)} fusion(bf16[128,4096]{1,0:T(8,128)(2,1)} %collective-permute-done.1, bf16[128,4096]{1,0:T(8,128)(2,1)S(1)} %get-tuple-element.5), kind=kLoop, calls=%fused_computation.1 | loop fusion | flops 2097152 | bytes 3145728 | tf_op jit(solution)/shard_map/convert_element_type | solution.py:303
  42.8 3.7 %all-to-all-start.2 = ((bf16[8,16,4096]{2,1,0:T(8,128)(2,1)}), bf16[8,16,4096]{2,1,0:T(8,128)(2,1)S(1)}, u32[]{:S(2)}, u32[]{:S(2)}) async-start(bf16[8,16,4096]{2,1,0:T(8,128)(2,1)} %bitcast.51), calls=%async_computation.2 | async-start | bytes 2097152 | tf_op jit(solution)/shard_map/all_to_all | solution.py:304
  47.4 1.1 %compare_select_fusion.1 = (bf16[384,128]{1,0:T(8,128)(2,1)S(1)}, bf16[384,128]{1,0:T(8,128)(2,1)S(1)}) fusion(bf16[1,384,128]{2,1,0:T(8,128)(2,1)} %constant.79, bf16[1,384,128]{2,1,0:T(8,128)(2,1)} %constant.78, s32[128]{0:T(128)S(1)} %copy-done.14, s32[384]{0:T(512)S(1)} %select_reduce_fusion.4, pred[]{:T(512)S(6)} %eq.194), kind=kLoop, calls=%fused_computation.8 | loop fusion | flops 245760 | bytes 395265 | tf_op jit(solution)/shard_map/jit(_where)/select_n | solution.py:315
  48.5 1.9 %copy-done.3 = bf16[4,1536,256]{2,1,0:T(8,128)(2,1)S(1)} copy-done((bf16[4,1536,256]{2,1,0:T(8,128)(2,1)S(1)}, bf16[4,1536,256]{2,1,0:T(8,128)(2,1)}, u32[]{:S(2)}) %copy-start.3) | copy-done | bytes 3145752
  50.4 4.9 %slot_scores.1 = f32[4,64,128]{2,1,0:T(8,128)S(1)} custom-call(s32[1]{0:T(128)} %bitcast.4.count_ref, bf16[4,1536,256]{2,1,0:T(8,128)(2,1)S(1)} %copy-done.3, bf16[384,128]{1,0:T(8,128)(2,1)S(1)} %get-tuple-element.9.pick_own_ref, bf16[384,128]{1,0:T(8,128)(2,1)S(1)} %get-tuple-element.8.pick_other_ref, bf16[128,4096]{1,0:T(8,128)(2,1)S(1)} %bitcast.49, ...), custom_call_target="tpu_custom_call" | custom-call | tf_op jit(solution)/shard_map/slot_scores/pallas_call | solution.py:321
  55.5 8.3 %all-to-all-done.2 = bf16[8,16,4096]{2,1,0:T(8,128)(2,1)S(1)} async-done(((bf16[8,16,4096]{2,1,0:T(8,128)(2,1)}), bf16[8,16,4096]{2,1,0:T(8,128)(2,1)S(1)}, u32[]{:S(2)}, u32[]{:S(2)}) %all-to-all-start.2) | async-done | bytes 1048608 | tf_op jit(solution)/shard_map/all_to_all | solution.py:304
  63.8 0.6 tile.19
  64.5 4.1 %all-to-all-start.1 = ((f32[8,4,512]{2,1,0:T(4,128)}), f32[8,4,512]{2,1,0:T(4,128)S(1)}, u32[]{:S(2)}, u32[]{:S(2)}) async-start(f32[8,4,512]{2,1,0:T(4,128)} %tile.19), calls=%async_computation.1 | async-start | bytes 131072 | tf_op jit(solution)/shard_map/all_to_all | solution.py:359
  68.6 2.2 %copy-done.1 = bf16[2048,1024]{1,0:T(8,128)(2,1)S(1)} copy-done((bf16[2048,1024]{1,0:T(8,128)(2,1)S(1)}, bf16[2048,1024]{1,0:T(8,128)(2,1)}, u32[]{:S(2)}) %copy-start.1) | copy-done | bytes 4194328
  70.8 2.3 %yz_planes.1 = bf16[1024,128]{1,0:T(8,128)(2,1)} custom-call(bf16[128,4096]{1,0:T(8,128)(2,1)S(1)} %bitcast.50, bf16[128,256]{1,0:T(8,128)(2,1)S(1)} %copy-done.7, bf16[2048,1024]{1,0:T(8,128)(2,1)S(1)} %copy-done.1), custom_call_target="tpu_custom_call" | custom-call | tf_op jit(solution)/shard_map/yz_planes/pallas_call | solution.py:366
  73.1 0.7 all-to-all-done.1
  73.8 5.6 %all-to-all-start.3 = ((bf16[16,64,128]{2,1,0:T(8,128)(2,1)}), bf16[16,64,128]{2,1,0:T(8,128)(2,1)S(1)}, u32[]{:S(2)}, u32[]{:S(2)}) async-start(bf16[16,64,128]{2,1,0:T(8,128)(2,1)} %bitcast.16), calls=%async_computation.3 | async-start | bytes 524288 | tf_op jit(solution)/shard_map/all_to_all | solution.py:374
  79.5 0.7 select_reduce_fusion
  80.3 7.9 %all-to-all-done.3.rows_ref = bf16[16,64,128]{2,1,0:T(8,128)(2,1)S(1)} async-done(((bf16[16,64,128]{2,1,0:T(8,128)(2,1)}), bf16[16,64,128]{2,1,0:T(8,128)(2,1)S(1)}, u32[]{:S(2)}, u32[]{:S(2)}) %all-to-all-start.3) | async-done | bytes 262176 | tf_op jit(solution)/shard_map/all_to_all | solution.py:374
  88.1 1.6 %x_rows.1 = f32[4,4,64,128]{3,2,1,0:T(8,128)} custom-call(bf16[16,64,128]{2,1,0:T(8,128)(2,1)S(1)} %all-to-all-done.3.rows_ref, bf16[4,256,256]{2,1,0:T(8,128)(2,1)S(1)} %copy-done.4), custom_call_target="tpu_custom_call" | custom-call | tf_op jit(solution)/shard_map/x_rows/pallas_call | solution.py:375
  (44 shorter events, 1.5 us)
Async XLA Ops:
  0.6 12.7 %copy-start.10 = (bf16[4,4,4096]{2,1,0:T(4,128)(2,1)S(1)}, bf16[4,4,4096]{2,1,0:T(4,128)(2,1)}, u32[]{:S(2)}) copy-start(bf16[4,4,4096]{2,1,0:T(4,128)(2,1)} %param.23) | copy-start | bytes 393220
  7.8 14.4 %copy-start.12 = (s32[512]{0:T(512)S(1)}, s32[512]{0:T(512)}, u32[]{:S(2)}) copy-start(s32[512]{0:T(512)} %constant.62.clone) | copy-start | bytes 6148
  7.8 14.4 %copy-start.14 = (s32[128]{0:T(128)S(1)}, s32[128]{0:T(128)}, u32[]{:S(2)}) copy-start(s32[128]{0:T(128)} %constant.60.clone) | copy-start | bytes 1540
  7.8 14.5 %copy-start.9 = (bf16[384,512]{1,0:T(8,128)(2,1)S(1)}, bf16[384,512]{1,0:T(8,128)(2,1)}, u32[]{:S(2)}) copy-start(bf16[384,512]{1,0:T(8,128)(2,1)} %constant.64.clone) | copy-start | bytes 1179652
  7.8 14.5 %copy-start.13 = (s32[384]{0:T(512)S(1)}, s32[384]{0:T(512)}, u32[]{:S(2)}) copy-start(s32[384]{0:T(512)} %constant.63.clone) | copy-start | bytes 4612
  7.8 14.7 %copy-start.5 = (bf16[256,256]{1,0:T(8,128)(2,1)S(1)}, bf16[256,256]{1,0:T(8,128)(2,1)}, u32[]{:S(2)}) copy-start(bf16[256,256]{1,0:T(8,128)(2,1)} %constant.65.clone.table_ref) | copy-start | bytes 393220
  11.9 28.5 %collective-permute-start.1 = (bf16[128,4096]{1,0:T(8,128)(2,1)}, bf16[128,4096]{1,0:T(8,128)(2,1)}, u32[]{:S(2)}, u32[]{:S(2)}) collective-permute-start(bf16[128,4096]{1,0:T(8,128)(2,1)} %convolution_convert_fusion), channel_id=1, source_target_pairs={{0,8},{8,0},{16,24},{24,16},{32,40},{40,32},{48,56},{56,48},{64,72... | collective-permute-start | bytes 3145736 | tf_op jit(solution)/shard_map/ppermute | solution.py:272
  14.4 24.8 %all-to-all-start = ((bf16[8,16,4096]{2,1,0:T(8,128)(2,1)}), bf16[8,16,4096]{2,1,0:T(8,128)(2,1)S(1)}, u32[]{:S(2)}, u32[]{:S(2)}) async-start(bf16[8,16,4096]{2,1,0:T(8,128)(2,1)} %tile.17), calls=%async_computation | async-start | bytes 2097152 | tf_op jit(solution)/shard_map/all_to_all | solution.py:236
  22.5 2.2 %copy-start = (bf16[8,64,4096]{2,1,0:T(8,128)(2,1)S(1)}, bf16[8,64,4096]{2,1,0:T(8,128)(2,1)}, u32[]{:S(2)}) copy-start(bf16[8,64,4096]{2,1,0:T(8,128)(2,1)} %param.22) | copy-start | bytes 12582916
  24.7 21.8 %copy-start.11 = (s32[8,1]{0,1:T(1,128)S(1)}, s32[8,1]{0,1:T(1,128)}, u32[]{:S(2)}) copy-start(s32[8,1]{0,1:T(1,128)} %param.24) | copy-start | bytes 100
  24.7 22.5 %copy-start.16 = (s32[8]{0:T(128)S(1)}, s32[8]{0:T(128)}, u32[]{:S(2)}) copy-start(s32[8]{0:T(128)} %param.25) | copy-start | bytes 100
  24.7 23.8 %copy-start.6 = (bf16[512,128]{1,0:T(8,128)(2,1)S(1)}, bf16[512,128]{1,0:T(8,128)(2,1)}, u32[]{:S(2)}) copy-start(bf16[512,128]{1,0:T(8,128)(2,1)} %constant.68.clone.wz_ref) | copy-start | bytes 393220
  24.7 23.8 %copy-start.8 = (bf16[16,40]{1,0:T(8,128)(2,1)S(1)}, bf16[16,40]{1,0:T(8,128)(2,1)}, u32[]{:S(2)}) copy-start(bf16[16,40]{1,0:T(8,128)(2,1)} %constant.67.clone.ex_ref) | copy-start | bytes 3844
  30.3 1.7 %copy-start.2 = (bf16[4,1536,256]{2,1,0:T(8,128)(2,1)}, bf16[4,1536,256]{2,1,0:T(8,128)(2,1)S(1)}, u32[]{:S(2)}) copy-start(bf16[4,1536,256]{2,1,0:T(8,128)(2,1)S(1)} %get-tuple-element.4.zp_ref) | copy-start | bytes 9437188
  39.2 9.2 %collective-permute-start = (bf16[128,4096]{1,0:T(8,128)(2,1)S(1)}, bf16[128,4096]{1,0:T(8,128)(2,1)S(1)}, u32[]{:S(2)}, u32[]{:S(2)}) collective-permute-start(bf16[128,4096]{1,0:T(8,128)(2,1)S(1)} %bitcast.48), channel_id=1, source_target_pairs={{0,8},{8,0},{16,24},{24,16},{32,40},{40,32},{48,56},{56,48},{64,72... | collective-permute-start | bytes 3145736 | tf_op jit(solution)/shard_map/ppermute | solution.py:239
  42.8 25.8 %copy-start.7 = (bf16[128,256]{1,0:T(8,128)(2,1)S(1)}, bf16[128,256]{1,0:T(8,128)(2,1)}, u32[]{:S(2)}) copy-start(bf16[128,256]{1,0:T(8,128)(2,1)} %constant.69.clone.z_ref) | copy-start | bytes 196612
  42.8 21.0 %all-to-all-start.2 = ((bf16[8,16,4096]{2,1,0:T(8,128)(2,1)}), bf16[8,16,4096]{2,1,0:T(8,128)(2,1)S(1)}, u32[]{:S(2)}, u32[]{:S(2)}) async-start(bf16[8,16,4096]{2,1,0:T(8,128)(2,1)} %bitcast.51), calls=%async_computation.2 | async-start | bytes 2097152 | tf_op jit(solution)/shard_map/all_to_all | solution.py:304
  48.5 1.9 %copy-start.3 = (bf16[4,1536,256]{2,1,0:T(8,128)(2,1)S(1)}, bf16[4,1536,256]{2,1,0:T(8,128)(2,1)}, u32[]{:S(2)}) copy-start(bf16[4,1536,256]{2,1,0:T(8,128)(2,1)} %copy-done.2) | copy-start | bytes 9437188
  55.3 24.1 %copy-start.15 = (s32[8]{0:T(128)S(1)}, s32[8]{0:T(128)}, u32[]{:S(2)}) copy-start(s32[8]{0:T(128)} %get-tuple-element.10) | copy-start | bytes 100
  55.3 32.8 %copy-start.4 = (bf16[4,256,256]{2,1,0:T(8,128)(2,1)S(1)}, bf16[4,256,256]{2,1,0:T(8,128)(2,1)}, u32[]{:S(2)}) copy-start(bf16[4,256,256]{2,1,0:T(8,128)(2,1)} %constant.71.clone.table_ref) | copy-start | bytes 1572868
  64.5 9.4 %all-to-all-start.1 = ((f32[8,4,512]{2,1,0:T(4,128)}), f32[8,4,512]{2,1,0:T(4,128)S(1)}, u32[]{:S(2)}, u32[]{:S(2)}) async-start(f32[8,4,512]{2,1,0:T(4,128)} %tile.19), calls=%async_computation.1 | async-start | bytes 131072 | tf_op jit(solution)/shard_map/all_to_all | solution.py:359
  68.6 2.2 %copy-start.1 = (bf16[2048,1024]{1,0:T(8,128)(2,1)S(1)}, bf16[2048,1024]{1,0:T(8,128)(2,1)}, u32[]{:S(2)}) copy-start(bf16[2048,1024]{1,0:T(8,128)(2,1)} %constant.70.clone.y_ref) | copy-start | bytes 12582916
  73.8 14.3 %all-to-all-start.3 = ((bf16[16,64,128]{2,1,0:T(8,128)(2,1)}), bf16[16,64,128]{2,1,0:T(8,128)(2,1)S(1)}, u32[]{:S(2)}, u32[]{:S(2)}) async-start(bf16[16,64,128]{2,1,0:T(8,128)(2,1)} %bitcast.16), calls=%async_computation.3 | async-start | bytes 524288 | tf_op jit(solution)/shard_map/all_to_all | solution.py:374

commit v2 on v1

--- a/solution.py
+++ b/solution.py
@@ -62,11 +62,9 @@
     return np.kron(np.eye(2), np.concatenate([c, -s], axis=1))
 
 
-def y_table(rows):
+def y_table():
     c, s = grid_cos_sin(np.arange(BOX), np.arange(BOX))
-    order = np.concatenate([np.arange(0, BOX, 2), np.arange(1, BOX, 2)])
-    both = np.concatenate([c[:, order], s[:, order]], axis=0)
-    return np.kron(both, np.eye(rows))
+    return np.concatenate([c, s], axis=0)
 
 
 def x_rows_table():
@@ -92,12 +90,82 @@
 
 STEP = 8
 CHUNK = 4
-
-
-def front_kernel(own_ref, pick_ref, flat_ref, table_ref, own_out, spectra_out):
-    flat = flat_ref[...]
-    own_out[...] = jnp.dot(own_ref[...], flat, preferred_element_type=F32).astype(BF)
-    along_x = jnp.dot(pick_ref[...], flat, preferred_element_type=F32).astype(BF)
+STEPS = PAIRS // CHUNK
+PLANES = BOX // DOM
+PER_CHIP = ROT_CLS * PLANES
+SEND = CHIPS * PER_CHIP
+
+
+def send_kernel(
+    class_ref,
+    rot_ref,
+    bucket_ref,
+    live_ref,
+    level_ref,
+    x_ref,
+    x_ref_table,
+    flat_ref,
+    send_out,
+    spread_out,
+    pick_out,
+    pick_own_out,
+    pick_other_out,
+    count_out,
+    spread_s,
+):
+    particles, columns = class_ref.shape[0], flat_ref.shape[0]
+
+    @pl.when(pl.program_id(0) == 0)
+    def _():
+        owner = lax.axis_index("rot")
+        core = lax.axis_index("dom") & 1
+        lane = lax.broadcasted_iota(jnp.int32, (1, columns), 1)
+        col_particle, col_x = lane >> 6, lane & (BOX - 1)
+        count = jnp.int32(0)
+        col_slot = jnp.full((1, columns), -1, jnp.int32)
+        col_rot = jnp.full((1, columns), -1, jnp.int32)
+        col_bucket = jnp.full((1, columns), -1, jnp.int32)
+        slot_rot = [jnp.int32(-1) for _ in range(CAP)]
+        for p in range(particles):
+            mine = (class_ref[p, 0] == owner) & (p < live_ref[0])
+            here = (col_particle == p) & mine
+            col_slot = jnp.where(here, count, col_slot)
+            col_rot = jnp.where(here, rot_ref[p], col_rot)
+            col_bucket = jnp.where(here, bucket_ref[p], col_bucket)
+            for slot in range(CAP):
+                slot_rot[slot] = jnp.where(mine & (count == slot), rot_ref[p], slot_rot[slot])
+            count = count + mine.astype(jnp.int32)
+        count_out[0] = count
+        levels = level_ref[...].astype(F32)
+        col_weight = jnp.zeros((1, columns), F32)
+        for level in range(levels.shape[1]):
+            value = jnp.broadcast_to(levels[:, level : level + 1], (1, columns))
+            col_weight = jnp.where(col_bucket == level, value, col_weight)
+        row = lax.broadcasted_iota(jnp.int32, (SEND, columns), 0)
+        base = (row // PER_CHIP) * (2 * PLANES) + (row & (PLANES - 1))
+        right = ((row // PLANES) & (ROT_CLS - 1)) == col_rot
+        for to_core, ref in ((core, spread_out), (1 - core, spread_s)):
+            hit = right & (base + to_core * PLANES == col_x)
+            ref[...] = jnp.where(hit, col_weight, 0.0).astype(BF)
+        ref_lane = lax.broadcasted_iota(jnp.int32, (1, SEND), 1)
+        ref_rot = (ref_lane // PLANES) & (ROT_CLS - 1)
+        for slot in range(CAP):
+            rows = slice(slot * 2 * KXP, (slot + 1) * 2 * KXP)
+            pick_out[rows] = jnp.where(col_slot == slot, x_ref[...], 0.0).astype(BF)
+            wanted = ref_rot == slot_rot[slot]
+            pick_own_out[rows] = jnp.where(wanted, x_ref_table[core], 0.0).astype(BF)
+            pick_other_out[rows] = jnp.where(wanted, x_ref_table[1 - core], 0.0).astype(BF)
+
+    send_out[...] = jnp.dot(spread_s[...], flat_ref[...], preferred_element_type=F32).astype(BF)
+
+
+def own_kernel(spread_ref, flat_ref, other_ref, out_ref):
+    own = jnp.dot(spread_ref[...], flat_ref[...], preferred_element_type=F32)
+    out_ref[...] = (own + other_ref[...].astype(F32)).astype(BF)
+
+
+def spectra_kernel(pick_ref, flat_ref, table_ref, spectra_out):
+    along_x = jnp.dot(pick_ref[...], flat_ref[...], preferred_element_type=F32).astype(BF)
     table = table_ref[...]
     for slot in range(CAP):
         part = z_stage(along_x[slot * 2 * KXP : (slot + 1) * 2 * KXP], table, 0, CHUNK)
@@ -187,20 +255,27 @@
         out_ref[...] = jnp.zeros_like(out_ref)
 
 
-def yz_kernel(parts_ref, z_ref, y_ref, out_ref):
-    rows = parts_ref.shape[0] // CHIPS
-    total = parts_ref[0:rows].astype(F32)
+def yz_kernel(parts_ref, z_ref, y_ref, out_ref, z_s, g_s):
+    total = parts_ref[0:PER_CHIP].astype(F32)
     for chip in range(1, CHIPS):
-        total = total + parts_ref[chip * rows : (chip + 1) * rows].astype(F32)
+        total = total + parts_ref[chip * PER_CHIP : (chip + 1) * PER_CHIP].astype(F32)
     total = total.astype(BF)
     stacked = jnp.concatenate([total[:, 128 * j : 128 * (j + 1)] for j in range(PAIRS)], axis=0)
-    z_part = jnp.dot(stacked, z_ref[...], preferred_element_type=F32).astype(BF)
-    z_part = jnp.concatenate([z_part[:, :128], z_part[:, 128:]], axis=0)
-    y_part = jnp.dot(y_ref[...], z_part, preferred_element_type=F32)
-    half_rows = y_part.shape[0] // 2
-    turned = pltpu.roll(y_part[half_rows:], BOX, 1)
-    first = lax.broadcasted_iota(jnp.int32, turned.shape, 1) < BOX
-    out_ref[...] = (y_part[:half_rows] + jnp.where(first, turned, -turned)).astype(BF)
+    z_part = jnp.dot(stacked, z_ref[...], preferred_element_type=F32)
+    for j in range(PAIRS):
+        for half in range(2):
+            start = (2 * j + half) * PER_CHIP
+            z_s[start : start + PER_CHIP] = z_part[
+                j * PER_CHIP : (j + 1) * PER_CHIP, 128 * half : 128 * (half + 1)
+            ]
+    by_y = [z_s[pl.ds(n, BOX, stride=PER_CHIP), :].astype(BF) for n in range(PER_CHIP)]
+    y_part = jnp.dot(y_ref[...], jnp.concatenate(by_y, axis=1), preferred_element_type=F32)
+    first = lax.broadcasted_iota(jnp.int32, (BOX, 128), 1) < BOX
+    for n in range(PER_CHIP):
+        lanes = slice(128 * n, 128 * (n + 1))
+        turned = pltpu.roll(y_part[BOX:, lanes], BOX, 1)
+        g_s[pl.ds(n, BOX, stride=PER_CHIP), :] = y_part[:BOX, lanes] + jnp.where(first, turned, -turned)
+    out_ref[...] = g_s[...].astype(BF)
 
 
 def x_rows_kernel(rows_ref, table_ref, out_ref):
@@ -219,104 +294,111 @@
 
 VMEM = pl.BlockSpec(memory_space=pltpu.VMEM)
 SMEM = pl.BlockSpec(memory_space=pltpu.SMEM)
-PARAMS = pltpu.CompilerParams(vmem_limit_bytes=40 * 1024 * 1024)
+
+
+def params(mib):
+    return pltpu.CompilerParams(vmem_limit_bytes=mib * 1024 * 1024)
+
+
+def cost(flops, moved):
+    return pl.CostEstimate(flops=flops, bytes_accessed=moved, transcendentals=0)
 
 
 def shards(particles, references, part_class, part_rot, bucket, bucket_weights, live_count):
     block_size = particles.shape[0]
-    planes = references.shape[1]
     voxels = BOX * BOX
-    per_chip = ROT_CLS * planes
     columns = block_size * BOX
-    core = lax.axis_index("dom") % 2
-    owner = lax.axis_index("rot")
     to_other = [(i, i ^ 1) for i in range(DOM)]
 
-    mine_refs = references.reshape(per_chip, voxels)
+    mine_refs = jnp.tile(references.reshape(PER_CHIP, voxels), (CHIPS, 1))
+    mine_refs, part_class = lax.optimization_barrier((mine_refs, part_class))
     refs_own = lax.all_to_all(
-        jnp.tile(mine_refs, (CHIPS, 1)), "dom", 0, 0, tiled=True, axis_index_groups=SAME_CORE
+        mine_refs, "dom", 0, 0, tiled=True, axis_index_groups=SAME_CORE
     )
-    refs_other = lax.ppermute(refs_own, "dom", to_other)
-
-    rows_all = jnp.arange(block_size, dtype=jnp.int32)
-    classes = part_class[:, 0]
-    alive = rows_all < live_count[0]
-    same = (classes[:, None] == classes[None, :]) & alive[None, :]
-    rank = jnp.sum((same & (rows_all[None, :] < rows_all[:, None])).astype(jnp.int32), axis=1)
-    mine = (classes == owner) & alive
-    count = jnp.sum(mine.astype(jnp.int32)).reshape(1)
-    bucket_ids = jnp.arange(bucket_weights.shape[0], dtype=jnp.int32)
-    level = jnp.where(
-        bucket[:, None] == bucket_ids[None, :], bucket_weights[None, :].astype(F32), 0.0
-    )
-    weight = jnp.where(mine, jnp.sum(level, axis=1), 0.0)
-    slot_of = jnp.where(mine, rank, -1)
-
-    col = np.arange(columns)
-    col_is = jnp.asarray(col[None, :] // BOX == np.arange(block_size)[:, None])
-    col_weight = jnp.sum(jnp.where(col_is, weight[:, None], 0.0), axis=0)
-    col_rot = jnp.sum(jnp.where(col_is, part_rot[:, None], 0), axis=0)
-    col_slot = jnp.sum(jnp.where(col_is, slot_of[:, None], 0), axis=0)
 
     flat = particles.reshape(columns, voxels)
-    row = np.arange(CHIPS * per_chip)
-    row_chip, row_r, row_x = row // per_chip, (row // planes) % ROT_CLS, row % planes
-    row_r = jnp.asarray(row_r.astype(np.int32))
-
-    def spread(to_core):
-        want_x = jnp.asarray((row_chip * 2 * planes + row_x).astype(np.int32)) + to_core * planes
-        hit = want_x[:, None] == jnp.asarray((col % BOX).astype(np.int32))[None, :]
-        return jnp.where(hit & (row_r[:, None] == col_rot[None, :]), col_weight[None, :], 0.0).astype(BF)
-
-    to_send = jnp.dot(spread(1 - core), flat, preferred_element_type=F32).astype(BF)
-    other = lax.ppermute(to_send, "dom", to_other)
-
     x_half = x_half_table()
-    slot_rows = np.arange(CAP * 2 * KXP) // (2 * KXP)
-    slot_rows = jnp.asarray(slot_rows.astype(np.int32))
-    pick = jnp.where(
-        slot_rows[:, None] == col_slot[None, :],
-        jnp.asarray(np.tile(x_half, (CAP, block_size)).astype(BF)),
-        jnp.zeros((), BF),
-    )
-    z_table = jnp.asarray(z_complex_table().astype(BF))
-    own, spectra = pl.pallas_call(
-        front_kernel,
+    by_core = x_half.reshape(2 * KXP, CHIPS, 2, 1, PLANES)
+    by_core = np.broadcast_to(by_core, (2 * KXP, CHIPS, 2, ROT_CLS, PLANES))
+    by_core = by_core.transpose(2, 0, 1, 3, 4).reshape(2, 2 * KXP, SEND)
+
+    def whole(*shape):
+        return pl.BlockSpec(shape, lambda s: (0,) * len(shape))
+
+    lane_chunk = pl.BlockSpec((columns, 128 * CHUNK), lambda i: (0, i))
+    send_chunk = pl.BlockSpec((SEND, 128 * CHUNK), lambda i: (0, i))
+    to_send, spread_own, pick, pick_own, pick_other, count = pl.pallas_call(
+        send_kernel,
         out_shape=(
-            jax.ShapeDtypeStruct((CHIPS * per_chip, voxels), BF),
-            jax.ShapeDtypeStruct((CAP, PAIRS * KXP, 4 * BOX), BF),
+            jax.ShapeDtypeStruct((SEND, voxels), BF),
+            jax.ShapeDtypeStruct((SEND, columns), BF),
+            jax.ShapeDtypeStruct((CAP * 2 * KXP, columns), BF),
+            jax.ShapeDtypeStruct((CAP * 2 * KXP, SEND), BF),
+            jax.ShapeDtypeStruct((CAP * 2 * KXP, SEND), BF),
+            jax.ShapeDtypeStruct((1,), jnp.int32),
         ),
-        grid=(PAIRS // CHUNK,),
+        grid=(STEPS,),
         in_specs=[
-            pl.BlockSpec((CHIPS * per_chip, columns), lambda i: (0, 0)),
-            pl.BlockSpec((CAP * 2 * KXP, columns), lambda i: (0, 0)),
-            pl.BlockSpec((columns, 128 * CHUNK), lambda i: (0, i)),
-            pl.BlockSpec((4 * BOX, 4 * BOX), lambda i: (0, 0)),
+            SMEM,
+            SMEM,
+            SMEM,
+            SMEM,
+            whole(1, bucket_weights.shape[0]),
+            whole(2 * KXP, columns),
+            whole(2, 2 * KXP, SEND),
+            lane_chunk,
         ],
         out_specs=(
-            pl.BlockSpec((CHIPS * per_chip, 128 * CHUNK), lambda i: (0, i)),
-            pl.BlockSpec((CAP, CHUNK * KXP, 4 * BOX), lambda i: (0, i, 0)),
+            send_chunk,
+            whole(SEND, columns),
+            whole(CAP * 2 * KXP, columns),
+            whole(CAP * 2 * KXP, SEND),
+            whole(CAP * 2 * KXP, SEND),
+            SMEM,
         ),
-        compiler_params=PARAMS,
-        name="front",
-    )(spread(core), pick, flat, z_table)
-    pair_sum = (own.astype(F32) + other.astype(F32)).astype(BF)
+        scratch_shapes=[pltpu.VMEM((SEND, columns), BF)],
+        compiler_params=params(54),
+        cost_estimate=cost(1024, 1024),
+        name="send",
+    )(
+        part_class,
+        part_rot,
+        bucket,
+        live_count,
+        bucket_weights.reshape(1, -1),
+        jnp.asarray(np.tile(x_half, (1, block_size)), F32),
+        jnp.asarray(by_core, F32),
+        flat,
+    )
+    other = lax.ppermute(to_send, "dom", to_other)
+
+    z_table = jnp.asarray(z_complex_table().astype(BF))
+    spectra = pl.pallas_call(
+        spectra_kernel,
+        out_shape=jax.ShapeDtypeStruct((CAP, PAIRS * KXP, 4 * BOX), BF),
+        grid=(STEPS,),
+        in_specs=[whole(CAP * 2 * KXP, columns), lane_chunk, whole(4 * BOX, 4 * BOX)],
+        out_specs=pl.BlockSpec((CAP, CHUNK * KXP, 4 * BOX), lambda i: (0, i, 0)),
+        compiler_params=params(54),
+        cost_estimate=cost(1024, 1024),
+        name="spectra",
+    )(pick, flat, z_table)
+
+    pair_sum = pl.pallas_call(
+        own_kernel,
+        out_shape=jax.ShapeDtypeStruct((SEND, voxels), BF),
+        grid=(STEPS,),
+        in_specs=[whole(SEND, columns), lane_chunk, send_chunk],
+        out_specs=send_chunk,
+        compiler_params=params(50),
+        cost_estimate=cost(1024, 1024),
+        name="own",
+    )(spread_own, flat, other)
+    refs_own, spectra = lax.optimization_barrier((refs_own, spectra))
+    refs_other = lax.ppermute(refs_own, "dom", to_other)
     arrived = lax.all_to_all(pair_sum, "dom", 0, 0, tiled=True, axis_index_groups=SAME_CORE)
 
-    slot_ids = jnp.arange(CAP, dtype=jnp.int32)
-    slot_rot = jnp.sum(jnp.where(slot_of[None, :] == slot_ids[:, None], part_rot[None, :], 0), axis=1)
-    row_rot = jnp.sum(jnp.where(slot_rows[:, None] == slot_ids[None, :], slot_rot[None, :], 0), axis=1)
-    by_core = x_half.reshape(2 * KXP, CHIPS, 2, 1, planes)
-    by_core = np.broadcast_to(by_core, (2 * KXP, CHIPS, 2, ROT_CLS, planes))
-    by_core = by_core.transpose(2, 0, 1, 3, 4).reshape(2, 2 * KXP, CHIPS * per_chip)
-    by_core = jnp.asarray(np.tile(by_core, (1, CAP, 1)).astype(BF))
-    right = row_rot[:, None] == row_r[None, :]
-    pick_own = jnp.where(right, jnp.where(core == 0, by_core[0], by_core[1]), jnp.zeros((), BF))
-    pick_other = jnp.where(right, jnp.where(core == 0, by_core[1], by_core[0]), jnp.zeros((), BF))
     ex, wz = shift_tables()
-
-    def whole(*shape):
-        return pl.BlockSpec(shape, lambda s: (0,) * len(shape))
 
     slots = pl.pallas_call(
         score_kernel,
@@ -325,10 +407,10 @@
         in_specs=[
             SMEM,
             pl.BlockSpec((None, PAIRS * KXP, 4 * BOX), lambda s: (s, 0, 0)),
-            whole(CAP * 2 * KXP, CHIPS * per_chip),
-            whole(CAP * 2 * KXP, CHIPS * per_chip),
-            whole(CHIPS * per_chip, voxels),
-            whole(CHIPS * per_chip, voxels),
+            whole(CAP * 2 * KXP, SEND),
+            whole(CAP * 2 * KXP, SEND),
+            whole(SEND, voxels),
+            whole(SEND, voxels),
             whole(4 * BOX, 4 * BOX),
             whole(2 * SHIFTS, KXV),
             whole(8 * BOX, 128),
@@ -341,7 +423,8 @@
             pltpu.VMEM((PAIRS, KXV, 4 * BOX), F32),
             pltpu.VMEM((SHIFTS, KXV, 4 * BOX), F32),
         ],
-        compiler_params=PARAMS,
+        compiler_params=params(50),
+        cost_estimate=cost(1024, 1024),
         name="slot_scores",
     )(
         count,
@@ -357,29 +440,34 @@
     slot_scores = slots[:, :, :SHIFTS].reshape(CAP, SHIFTS, SHIFTS, SHIFTS)
     slot_scores = slot_scores.transpose(0, 2, 1, 3).reshape(CAP, SHIFTS**3)
     everywhere = lax.all_to_all(jnp.tile(slot_scores, (8, 1)), "rot", 0, 0, tiled=True)
-    place = classes * CAP + rank
+    rows_all = jnp.arange(block_size, dtype=jnp.int32)
+    classes = part_class[:, 0]
+    alive = rows_all < live_count[0]
+    before = (classes[:, None] == classes[None, :]) & (rows_all[None, :] < rows_all[:, None])
+    place = classes * CAP + jnp.sum(before.astype(jnp.int32), axis=1)
     found = (place[:, None] == jnp.arange(8 * CAP, dtype=jnp.int32)[None, :]) & alive[:, None]
     scores = jnp.sum(jnp.where(found[:, :, None], everywhere[None, :, :], 0.0), axis=1)
 
     z_real = jnp.asarray(z_real_table().astype(BF))
-    y_full = jnp.asarray(y_table(per_chip).astype(BF))
     grids = pl.pallas_call(
         yz_kernel,
-        out_shape=jax.ShapeDtypeStruct((BOX * per_chip, 2 * BOX), BF),
+        out_shape=jax.ShapeDtypeStruct((BOX * PER_CHIP, 2 * BOX), BF),
         in_specs=[VMEM] * 3,
         out_specs=VMEM,
-        compiler_params=PARAMS,
+        scratch_shapes=[pltpu.VMEM((BOX * PER_CHIP, 128), F32)] * 2,
+        compiler_params=params(50),
+        cost_estimate=cost(1024, 1024),
         name="yz_planes",
-    )(arrived, z_real, y_full)
+    )(arrived, z_real, jnp.asarray(y_table().astype(BF)))
     by_rows = lax.all_to_all(grids, "dom", 0, 0, tiled=True)
     sums = pl.pallas_call(
         x_rows_kernel,
         out_shape=jax.ShapeDtypeStruct((BOX // DOM, ROT_CLS, BOX, 2 * BOX), F32),
         in_specs=[VMEM] * 2,
         out_specs=VMEM,
-        compiler_params=PARAMS,
+        compiler_params=params(50),
         name="x_rows",
-    )(by_rows.reshape(DOM, BOX // DOM * per_chip, 2 * BOX), jnp.asarray(x_rows_table()))
+    )(by_rows.reshape(DOM, PLANES * PER_CHIP, 2 * BOX), jnp.asarray(x_rows_table()))
     return (scores, sums)
 
 

time: 90.4 us -> 88.9 us (0.983)
  Pallas kernels: 14.4 us -> 34.8 us
  other arithmetic: 11.9 us -> 1.01 us
  waiting for transfers between devices: 24.2 us -> 16.4 us
  matrix products: 4.01 us -> 0 us
  starting transfers between devices: 23.7 us -> 27.2 us
  local copies, waits for them, and re-layouts: 9.9 us -> 7.02 us
    pallas_call x2 -> x4, Pallas kernels: 7.87 us -> 23.7 us  [the longest x1 8.43 us: shards(): pl.pallas_call(spectra_kernel, out_shape=jax.ShapeDtypeStruct((CAP, PAIRS...]
    all_to_all x1, waiting for transfers between devices: 7.31 us -> 0.01 us  [shards(): lax.all_to_all(mine_refs, 'dom', 0, 0, tiled=True, axis_index_groups=SAME...]
    unnamed x34 -> x20, local copies, waits for them, and re-layouts: 7.95 us -> 2.85 us
    pallas_call x1, Pallas kernels: 4.95 us -> 9.51 us  [shards(): pl.pallas_call(score_kernel, out_shape=jax.ShapeDtypeStruct((CAP, SHIFTS...]
    dot_general x1 -> x0, matrix products: 4.01 us -> none  [shards(): jnp.dot(spread(1 - core), flat, preferred_element_type=F32).astype(BF)]
    all_to_all x1, waiting for transfers between devices: 8.32 us -> 4.83 us  [shards(): lax.all_to_all(pair_sum, 'dom', 0, 0, tiled=True, axis_index_groups=SAME_...]
    all_to_all x1, starting transfers between devices: 3.69 us -> 7.06 us  [shards(): lax.all_to_all(pair_sum, 'dom', 0, 0, tiled=True, axis_index_groups=SAME_...]
    reduce_sum x6 -> x1, other arithmetic: 3.5 us -> 0.18 us  [shards(): place = classes * CAP + jnp.sum(before.astype(jnp.int32), axis=1)]
  transfers between devices with their start and end apart: 6 -> 6, of which waited for: 4 -> 3; matrix products, arithmetic and copies ran while one was open for 8% -> 3% of each run, Pallas kernels for 14% -> 30%
where the time goes in v2:
time: 88.9 us; the launch traced here: 87.8 us
  Pallas kernels  34.8 us (39%)
  starting transfers between devices  27.2 us (31%)
  waiting for transfers between devices  16.4 us (18%)
  local copies, waits for them, and re-layouts  7.02 us (8%)
  between operations  1.4 us (2%)
  other arithmetic  1.01 us (1%)
    pallas_call x1, Pallas kernels, shards(): pl.pallas_call(score_kernel, out_shape=jax.ShapeDtypeStruct((CAP, SHIFTS...  9.51 us
    all_to_all x1, starting transfers between devices, shards(): lax.all_to_all(mine_refs, 'dom', 0, 0, tiled=True, axis_index_groups=SAME...  8.49 us
    pallas_call x1, Pallas kernels, shards(): pl.pallas_call(spectra_kernel, out_shape=jax.ShapeDtypeStruct((CAP, PAIRS...  8.43 us
    all_to_all x1, waiting for transfers between devices, shards(): by_rows = lax.all_to_all(grids, 'dom', 0, 0, tiled=True)  7.89 us
    pallas_call x1, Pallas kernels, shards(): pl.pallas_call(send_kernel, out_shape=(jax.ShapeDtypeStruct((SEND, voxels...  7.08 us
    all_to_all x1, starting transfers between devices, shards(): lax.all_to_all(pair_sum, 'dom', 0, 0, tiled=True, axis_index_groups=SAME_...  7.06 us
    pallas_call x1, Pallas kernels, shards(): pl.pallas_call(own_kernel, out_shape=jax.ShapeDtypeStruct((SEND, voxels),...  6.74 us
    all_to_all x1, starting transfers between devices, shards(): by_rows = lax.all_to_all(grids, 'dom', 0, 0, tiled=True)  6.41 us
  transfers between devices with their start and end apart: 6, of which 3 were waited for; matrix products, arithmetic and copies ran while one was open for 3% of the time, Pallas kernels for 30%

profile of v2, /device:TPU:1, one launch (start us, length us, event | category | flops | bytes accessed | tf_op | source)
XLA Modules:
  0.0 87.8 jit_solution(14200475140234200855)
XLA Ops:
  0.6 0.9 %tile.18 = bf16[16,4096]{1,0:T(8,128)(2,1)S(1)} reshape(bf16[4,4,4096]{2,1,0:T(4,128)(2,1)} %param.16) | data formatting | bytes 262144 | tf_op jit(solution)/shard_map/tile | solution.py:313
  1.6 1.1 %tile.19 = bf16[8,16,4096]{2,1,0:T(8,128)(2,1)} broadcast(bf16[16,4096]{1,0:T(8,128)(2,1)S(1)} %tile.18), dimensions={1,2} | broadcast | bytes 1179648 | tf_op jit(solution)/shard_map/tile | solution.py:313
  2.7 8.5 %all-to-all-start = ((bf16[8,16,4096]{2,1,0:T(8,128)(2,1)}), bf16[8,16,4096]{2,1,0:T(8,128)(2,1)S(1)}, u32[]{:S(2)}, u32[]{:S(2)}) async-start(bf16[8,16,4096]{2,1,0:T(8,128)(2,1)} %bitcast.7), calls=%async_computation | async-start | bytes 2097152 | tf_op jit(solution)/shard_map/all_to_all | solution.py:315
  11.8 1.3 %copy.20.class_ref = s32[8,1]{1,0:T(8,128)} copy(s32[8,1]{0,1:T(1,128)} %param.17) | data formatting | bytes 64 | tf_op jit(solution)/shard_map/optimization_barrier | solution.py:314
  13.1 7.1 %send.1 = (bf16[128,4096]{1,0:T(8,128)(2,1)}, bf16[128,512]{1,0:T(8,128)(2,1)}, bf16[384,512]{1,0:T(8,128)(2,1)}, bf16[384,128]{1,0:T(8,128)(2,1)}, bf16[384,128]{1,0:T(8,128)(2,1)}, /*index=5*/s32[1]{0:T(128)}) custom-call(s32[8,1]{1,0:T(8,128)} %copy.20.class_ref, s32[8]{0:T(128)} %rot_ref.1, s32[8]{0:T(128)} %bucket_ref.1, s32[1]{0:T(128)} %copy.24.live_ref, ...), custom_call_target="tpu_custom_call" | custom-call | flops 1024 | bytes 1024 | tf_op jit(solution)/shard_map/send/pallas_call | solution.py:330
  20.2 1.0 %collective-permute-start.1 = (bf16[128,4096]{1,0:T(8,128)(2,1)}, bf16[128,4096]{1,0:T(8,128)(2,1)S(1)}, u32[]{:S(2)}, u32[]{:S(2)}) collective-permute-start(bf16[128,4096]{1,0:T(8,128)(2,1)} %get-tuple-element.21), channel_id=1, source_target_pairs={{0,8},{8,0},{16,24},{24,16},{32,40},{40,32},{48,56},{56,48},{64,72... | collective-permute-start | bytes 3145736 | tf_op jit(solution)/shard_map/ppermute | solution.py:373
  21.3 8.4 %spectra.1.zp_ref = bf16[4,1536,256]{2,1,0:T(8,128)(2,1)} custom-call(bf16[384,512]{1,0:T(8,128)(2,1)} %get-tuple-element.15.pick_ref, bf16[512,4096]{1,0:T(8,128)(2,1)} %bitcast.28, bf16[256,256]{1,0:T(8,128)(2,1)} %constant.24.clone.table_ref), custom_call_target="tpu_custom_call" | custom-call | flops 1024 | bytes 1024 | tf_op jit(solution)/shard_map/spectra/pallas_call | solution.py:376
  29.7 0.0 all-to-all-done
  29.7 0.0 collective-permute-start
  29.7 0.0 collective-permute-done.1.other_ref
  29.8 0.0 copy-start.3
  29.8 0.0 copy-start.8
  29.8 6.7 %own.1 = bf16[128,4096]{1,0:T(8,128)(2,1)} custom-call(bf16[128,512]{1,0:T(8,128)(2,1)S(1)} %copy-done.2, bf16[512,4096]{1,0:T(8,128)(2,1)} %bitcast.29, bf16[128,4096]{1,0:T(8,128)(2,1)S(1)} %collective-permute-done.1.other_ref), custom_call_target="tpu_custom_call" | custom-call | flops 1024 | bytes 1024 | tf_op jit(solution)/shard_map/own/pallas_call | solution.py:387
  36.5 7.1 %all-to-all-start.2 = ((bf16[8,16,4096]{2,1,0:T(8,128)(2,1)}), bf16[8,16,4096]{2,1,0:T(8,128)(2,1)S(1)}, u32[]{:S(2)}, u32[]{:S(2)}) async-start(bf16[8,16,4096]{2,1,0:T(8,128)(2,1)} %bitcast.11), calls=%async_computation.2 | async-start | bytes 2097152 | tf_op jit(solution)/shard_map/all_to_all | solution.py:399
  43.6 0.0 copy-done.9
  43.6 0.2 convert_reduce_fusion
  43.8 0.0 collective-permute-done.other_ref
  43.8 0.9 %copy-done.4 = bf16[384,128]{1,0:T(8,128)(2,1)S(1)} copy-done((bf16[384,128]{1,0:T(8,128)(2,1)S(1)}, bf16[384,128]{1,0:T(8,128)(2,1)}, u32[]{:S(2)}) %copy-start.4) | copy-done | bytes 98328
  44.7 0.9 %copy-done.5 = bf16[384,128]{1,0:T(8,128)(2,1)S(1)} copy-done((bf16[384,128]{1,0:T(8,128)(2,1)S(1)}, bf16[384,128]{1,0:T(8,128)(2,1)}, u32[]{:S(2)}) %copy-start.5) | copy-done | bytes 98328
  45.6 9.5 %slot_scores.1 = f32[4,64,128]{2,1,0:T(8,128)S(1)} custom-call(s32[1]{0:T(128)} %get-tuple-element.13.count_ref, bf16[4,1536,256]{2,1,0:T(8,128)(2,1)} %spectra.1.zp_ref, bf16[384,128]{1,0:T(8,128)(2,1)S(1)} %copy-done.4, bf16[384,128]{1,0:T(8,128)(2,1)S(1)} %copy-done.5, bf16[128,4096]{1,0:T(8,128)(2,1)S(1)} %bitcast.26, ...), custom_call_target="tpu_custom_call" | custom-call | flops 1024 | bytes 1024 | tf_op jit(solution)/shard_map/slot_scores/pallas_call | solution.py:403
  55.2 0.1 tile.21
  55.3 4.8 %all-to-all-done.2 = bf16[8,16,4096]{2,1,0:T(8,128)(2,1)S(1)} async-done(((bf16[8,16,4096]{2,1,0:T(8,128)(2,1)}), bf16[8,16,4096]{2,1,0:T(8,128)(2,1)S(1)}, u32[]{:S(2)}, u32[]{:S(2)}) %all-to-all-start.2) | async-done | bytes 1048608 | tf_op jit(solution)/shard_map/all_to_all | solution.py:399
  60.1 0.6 tile.22
  60.7 4.1 %all-to-all-start.1 = ((f32[8,4,512]{2,1,0:T(4,128)}), f32[8,4,512]{2,1,0:T(4,128)S(1)}, u32[]{:S(2)}, u32[]{:S(2)}) async-start(f32[8,4,512]{2,1,0:T(4,128)} %tile.22), calls=%async_computation.1 | async-start | bytes 131072 | tf_op jit(solution)/shard_map/all_to_all | solution.py:442
  64.9 1.5 %yz_planes.1 = bf16[1024,128]{1,0:T(8,128)(2,1)} custom-call(bf16[128,4096]{1,0:T(8,128)(2,1)S(1)} %bitcast.24, bf16[128,256]{1,0:T(8,128)(2,1)S(1)} %copy-done.6, bf16[128,64]{1,0:T(8,128)(2,1)S(1)} %copy-done.7), custom_call_target="tpu_custom_call" | custom-call | flops 1024 | bytes 1024 | tf_op jit(solution)/shard_map/yz_planes/pallas_call | solution.py:452
  66.4 3.7 %all-to-all-done.1 = f32[8,4,512]{2,1,0:T(4,128)S(1)} async-done(((f32[8,4,512]{2,1,0:T(4,128)}), f32[8,4,512]{2,1,0:T(4,128)S(1)}, u32[]{:S(2)}, u32[]{:S(2)}) %all-to-all-start.1) | async-done | bytes 65568 | tf_op jit(solution)/shard_map/all_to_all | solution.py:442
  70.1 6.4 %all-to-all-start.3 = ((bf16[16,64,128]{2,1,0:T(8,128)(2,1)}), bf16[16,64,128]{2,1,0:T(8,128)(2,1)S(1)}, u32[]{:S(2)}, u32[]{:S(2)}) async-start(bf16[16,64,128]{2,1,0:T(8,128)(2,1)} %bitcast.13), calls=%async_computation.3 | async-start | bytes 524288 | tf_op jit(solution)/shard_map/all_to_all | solution.py:462
  76.5 0.1 fusion.1
  76.6 0.7 select_reduce_fusion
  77.3 7.9 %all-to-all-done.3.rows_ref = bf16[16,64,128]{2,1,0:T(8,128)(2,1)S(1)} async-done(((bf16[16,64,128]{2,1,0:T(8,128)(2,1)}), bf16[16,64,128]{2,1,0:T(8,128)(2,1)S(1)}, u32[]{:S(2)}, u32[]{:S(2)}) %all-to-all-start.3) | async-done | bytes 262176 | tf_op jit(solution)/shard_map/all_to_all | solution.py:462
  85.2 1.0 %copy-done.1 = bf16[4,256,256]{2,1,0:T(8,128)(2,1)S(1)} copy-done((bf16[4,256,256]{2,1,0:T(8,128)(2,1)S(1)}, bf16[4,256,256]{2,1,0:T(8,128)(2,1)}, u32[]{:S(2)}) %copy-start.1) | copy-done | bytes 524312
  86.3 1.6 %x_rows.1 = f32[4,4,64,128]{3,2,1,0:T(8,128)} custom-call(bf16[16,64,128]{2,1,0:T(8,128)(2,1)S(1)} %all-to-all-done.3.rows_ref, bf16[4,256,256]{2,1,0:T(8,128)(2,1)S(1)} %copy-done.1), custom_call_target="tpu_custom_call" | custom-call | tf_op jit(solution)/shard_map/x_rows/pallas_call | solution.py:463
  (19 shorter events, 0.1 us)
Async XLA Ops:
  2.7 27.0 %all-to-all-start = ((bf16[8,16,4096]{2,1,0:T(8,128)(2,1)}), bf16[8,16,4096]{2,1,0:T(8,128)(2,1)S(1)}, u32[]{:S(2)}, u32[]{:S(2)}) async-start(bf16[8,16,4096]{2,1,0:T(8,128)(2,1)} %bitcast.7), calls=%async_computation | async-start | bytes 2097152 | tf_op jit(solution)/shard_map/all_to_all | solution.py:315
  20.2 9.5 %copy-start.2 = (bf16[128,512]{1,0:T(8,128)(2,1)S(1)}, bf16[128,512]{1,0:T(8,128)(2,1)}, u32[]{:S(2)}) copy-start(bf16[128,512]{1,0:T(8,128)(2,1)} %get-tuple-element.20.spread_ref) | copy-start | bytes 393220
  20.2 9.5 %collective-permute-start.1 = (bf16[128,4096]{1,0:T(8,128)(2,1)}, bf16[128,4096]{1,0:T(8,128)(2,1)S(1)}, u32[]{:S(2)}, u32[]{:S(2)}) collective-permute-start(bf16[128,4096]{1,0:T(8,128)(2,1)} %get-tuple-element.21), channel_id=1, source_target_pairs={{0,8},{8,0},{16,24},{24,16},{32,40},{40,32},{48,56},{56,48},{64,72... | collective-permute-start | bytes 3145736 | tf_op jit(solution)/shard_map/ppermute | solution.py:373
  29.7 14.1 %collective-permute-start = (bf16[128,4096]{1,0:T(8,128)(2,1)S(1)}, bf16[128,4096]{1,0:T(8,128)(2,1)S(1)}, u32[]{:S(2)}, u32[]{:S(2)}) collective-permute-start(bf16[128,4096]{1,0:T(8,128)(2,1)S(1)} %bitcast.25), channel_id=1, source_target_pairs={{0,8},{8,0},{16,24},{24,16},{32,40},{40,32},{48,56},{56,48},{64,72... | collective-permute-start | bytes 3145736 | tf_op jit(solution)/shard_map/ppermute | solution.py:398
  29.8 13.8 %copy-start.9 = (s32[8,1]{0,1:T(1,128)S(1)}, s32[8,1]{0,1:T(1,128)}, u32[]{:S(2)}) copy-start(s32[8,1]{0,1:T(1,128)} %param.17) | copy-start | bytes 100
  29.8 14.0 %copy-start = (bf16[256,256]{1,0:T(8,128)(2,1)S(1)}, bf16[256,256]{1,0:T(8,128)(2,1)}, u32[]{:S(2)}) copy-start(bf16[256,256]{1,0:T(8,128)(2,1)} %constant.24.clone.table_ref) | copy-start | bytes 393220
  29.8 14.0 %copy-start.3 = (bf16[512,128]{1,0:T(8,128)(2,1)S(1)}, bf16[512,128]{1,0:T(8,128)(2,1)}, u32[]{:S(2)}) copy-start(bf16[512,128]{1,0:T(8,128)(2,1)} %constant.26.clone.wz_ref) | copy-start | bytes 393220
  29.8 14.0 %copy-start.8 = (bf16[16,40]{1,0:T(8,128)(2,1)S(1)}, bf16[16,40]{1,0:T(8,128)(2,1)}, u32[]{:S(2)}) copy-start(bf16[16,40]{1,0:T(8,128)(2,1)} %constant.25.clone.ex_ref) | copy-start | bytes 3844
  36.5 28.4 %copy-start.6 = (bf16[128,256]{1,0:T(8,128)(2,1)S(1)}, bf16[128,256]{1,0:T(8,128)(2,1)}, u32[]{:S(2)}) copy-start(bf16[128,256]{1,0:T(8,128)(2,1)} %constant.27.clone.z_ref) | copy-start | bytes 196612
  36.5 28.4 %copy-start.7 = (bf16[128,64]{1,0:T(8,128)(2,1)S(1)}, bf16[128,64]{1,0:T(8,128)(2,1)}, u32[]{:S(2)}) copy-start(bf16[128,64]{1,0:T(8,128)(2,1)} %constant.28.clone.y_ref) | copy-start | bytes 49156
  36.5 23.6 %all-to-all-start.2 = ((bf16[8,16,4096]{2,1,0:T(8,128)(2,1)}), bf16[8,16,4096]{2,1,0:T(8,128)(2,1)S(1)}, u32[]{:S(2)}, u32[]{:S(2)}) async-start(bf16[8,16,4096]{2,1,0:T(8,128)(2,1)} %bitcast.11), calls=%async_computation.2 | async-start | bytes 2097152 | tf_op jit(solution)/shard_map/all_to_all | solution.py:399
  43.8 0.9 %copy-start.4 = (bf16[384,128]{1,0:T(8,128)(2,1)S(1)}, bf16[384,128]{1,0:T(8,128)(2,1)}, u32[]{:S(2)}) copy-start(bf16[384,128]{1,0:T(8,128)(2,1)} %get-tuple-element.17.pick_own_ref) | copy-start | bytes 294916
  44.7 0.9 %copy-start.5 = (bf16[384,128]{1,0:T(8,128)(2,1)S(1)}, bf16[384,128]{1,0:T(8,128)(2,1)}, u32[]{:S(2)}) copy-start(bf16[384,128]{1,0:T(8,128)(2,1)} %get-tuple-element.18.pick_other_ref) | copy-start | bytes 294916
  60.7 9.3 %all-to-all-start.1 = ((f32[8,4,512]{2,1,0:T(4,128)}), f32[8,4,512]{2,1,0:T(4,128)S(1)}, u32[]{:S(2)}, u32[]{:S(2)}) async-start(f32[8,4,512]{2,1,0:T(4,128)} %tile.22), calls=%async_computation.1 | async-start | bytes 131072 | tf_op jit(solution)/shard_map/all_to_all | solution.py:442
  70.1 15.1 %all-to-all-start.3 = ((bf16[16,64,128]{2,1,0:T(8,128)(2,1)}), bf16[16,64,128]{2,1,0:T(8,128)(2,1)S(1)}, u32[]{:S(2)}, u32[]{:S(2)}) async-start(bf16[16,64,128]{2,1,0:T(8,128)(2,1)} %bitcast.13), calls=%async_computation.3 | async-start | bytes 524288 | tf_op jit(solution)/shard_map/all_to_all | solution.py:462
  85.2 1.0 %copy-start.1 = (bf16[4,256,256]{2,1,0:T(8,128)(2,1)S(1)}, bf16[4,256,256]{2,1,0:T(8,128)(2,1)}, u32[]{:S(2)}) copy-start(bf16[4,256,256]{2,1,0:T(8,128)(2,1)} %constant.29.clone.table_ref) | copy-start | bytes 1572868

commit v3 on v2

v3 whole, which is shorter than its diff:
```python
import math

import jax
import jax.numpy as jnp
import numpy as np
from jax import lax
from jax.experimental import pallas as pl
from jax.experimental.pallas import tpu as pltpu
from jax.sharding import PartitionSpec as P

BOX = 64
SHIFTS = 8
ROT_CLS = 4
CAP = 4
HALF = 33
KXP = 48
KXV = 40
PAIRS = BOX // 2
DOM = 16
CHIPS = DOM // 2
SAME_CORE = [[2 * chip + core for chip in range(CHIPS)] for core in range(2)]
BF = jnp.bfloat16
F32 = jnp.float32


def grid_cos_sin(rows, cols):
    theta = ((rows[:, None] * cols[None, :]) % BOX).astype(np.float64) * (2.0 * math.pi / BOX)
    return np.cos(theta), np.sin(theta)


def x_half_table():
    c, s = grid_cos_sin(np.arange(BOX), np.arange(BOX))
    out = np.zeros((2, KXP, BOX))
    out[0, :HALF] = c[:HALF]
    out[1, :HALF] = -s[:HALF]
    return out.reshape(2 * KXP, BOX)


def z_complex_table():
    c, s = grid_cos_sin(np.arange(BOX), np.arange(BOX))
    two = np.eye(2)
    return np.block([[np.kron(two, c), np.kron(two, -s)], [np.kron(two, s), np.kron(two, c)]])


def shift_tables():
    c, s = grid_cos_sin(np.arange(SHIFTS) - SHIFTS // 2, np.arange(BOX))
    fold = np.zeros((KXV,))
    fold[:HALF] = 2.0
    fold[0] = fold[HALF - 1] = 1.0
    ex = np.zeros((2 * SHIFTS, KXV))
    ex[:SHIFTS, :HALF] = c[:, :HALF]
    ex[SHIFTS:, :HALF] = s[:, :HALF]
    ex = ex * fold[None, :]
    wz = np.zeros((2, 4 * BOX, 128))
    wz[0, :, :SHIFTS] = np.concatenate([c.T, c.T, -s.T, -s.T], axis=0)
    wz[1, :, :SHIFTS] = np.concatenate([-s.T, -s.T, -c.T, -c.T], axis=0)
    return ex, wz.reshape(8 * BOX, 128)


def z_real_table():
    c, s = grid_cos_sin(np.arange(BOX), np.arange(BOX))
    return np.kron(np.eye(2), np.concatenate([c, -s], axis=1))


def y_table():
    c, s = grid_cos_sin(np.arange(BOX), np.arange(BOX))
    return np.concatenate([c, s], axis=0)


def x_rows_table():
    c, s = grid_cos_sin(np.arange(BOX), np.arange(BOX))
    full = []
    for table in (c, s):
        spread = np.einsum(
            "rq,kdx->rkdqx", np.eye(ROT_CLS), table.reshape(BOX, DOM, BOX // DOM)
        ).reshape(ROT_CLS * BOX, ROT_CLS * BOX)
        high = spread.astype(np.float32).astype(BF)
        low = (spread.astype(np.float32) - high.astype(np.float32)).astype(BF)
        full += [high, low]
    return np.stack(full)


def z_stage(src, table, start, count):
    parts = []
    for j in range(start, start + count):
        lanes = slice(128 * j, 128 * (j + 1))
        parts.append(jnp.concatenate([src[0:KXP, lanes], src[KXP : 2 * KXP, lanes]], axis=1))
    return jnp.dot(jnp.concatenate(parts, axis=0), table, preferred_element_type=F32)


STEP = 8
CHUNK = 4
PLANES = BOX // DOM
PER_CHIP = ROT_CLS * PLANES
SEND = CHIPS * PER_CHIP


LANES = 1024


def send_kernel(
    class_ref,
    rot_ref,
    bucket_ref,
    live_ref,
    level_ref,
    x_ref,
    flat_hbm,
    send_out,
    own_out,
    pick_out,
    count_out,
    slot_rot_out,
    flat_s,
    spread_s,
    sems,
):
    particles, columns = class_ref.shape[0], flat_hbm.shape[0]
    copies = [
        pltpu.make_async_copy(
            flat_hbm.at[p * BOX : (p + 1) * BOX], flat_s.at[p * BOX : (p + 1) * BOX], sems.at[p]
        )
        for p in range(particles)
    ]
    for copy in copies:
        copy.start()
    owner = lax.axis_index("rot")
    core = lax.axis_index("dom") & 1
    lane = lax.broadcasted_iota(jnp.int32, (1, columns), 1)
    col_particle, col_x = lane >> 6, lane & (BOX - 1)
    count = jnp.int32(0)
    col_slot = jnp.full((1, columns), -1, jnp.int32)
    col_rot = jnp.full((1, columns), -1, jnp.int32)
    col_bucket = jnp.full((1, columns), -1, jnp.int32)
    slot_rot = [jnp.int32(-1) for _ in range(CAP)]
    for p in range(particles):
        mine = (class_ref[p] == owner) & (p < live_ref[0])
        here = (col_particle == p) & mine
        col_slot = jnp.where(here, count, col_slot)
        col_rot = jnp.where(here, rot_ref[p], col_rot)
        col_bucket = jnp.where(here, bucket_ref[p], col_bucket)
        for slot in range(CAP):
            slot_rot[slot] = jnp.where(mine & (count == slot), rot_ref[p], slot_rot[slot])
        count = count + mine.astype(jnp.int32)
    count_out[0] = count
    for slot in range(CAP):
        slot_rot_out[slot] = slot_rot[slot]
    levels = level_ref[...].astype(F32)
    col_weight = jnp.zeros((1, columns), F32)
    for level in range(levels.shape[1]):
        value = jnp.broadcast_to(levels[:, level : level + 1], (1, columns))
        col_weight = jnp.where(col_bucket == level, value, col_weight)
    row = lax.broadcasted_iota(jnp.int32, (SEND, columns), 0)
    base = (row // PER_CHIP) * (2 * PLANES) + (row & (PLANES - 1))
    right = ((row // PLANES) & (ROT_CLS - 1)) == col_rot
    for half, to_core in enumerate((core, 1 - core)):
        hit = right & (base + to_core * PLANES == col_x)
        spread_s[half * SEND : (half + 1) * SEND] = jnp.where(hit, col_weight, 0.0).astype(BF)
    for slot in range(CAP):
        rows = slice(slot * 2 * KXP, (slot + 1) * 2 * KXP)
        pick_out[rows] = jnp.where(col_slot == slot, x_ref[...], 0.0).astype(BF)
    for copy in copies:
        copy.wait()
    for start in range(0, BOX * BOX, LANES):
        lanes = slice(start, start + LANES)
        part = jnp.dot(spread_s[...], flat_s[:, lanes], preferred_element_type=F32)
        own_out[:, lanes] = part[:SEND].astype(BF)
        send_out[:, lanes] = part[SEND:].astype(BF)


def pair_kernel(own_ref, other_ref, out_ref):
    out_ref[...] = (own_ref[...].astype(F32) + other_ref[...].astype(F32)).astype(BF)


def spectra_kernel(pick_ref, flat_hbm, table_ref, spectra_out, flat_s, sems):
    particles = flat_hbm.shape[0] // BOX
    copies = [
        pltpu.make_async_copy(
            flat_hbm.at[p * BOX : (p + 1) * BOX], flat_s.at[p * BOX : (p + 1) * BOX], sems.at[p]
        )
        for p in range(particles)
    ]
    for copy in copies:
        copy.start()
    for copy in copies:
        copy.wait()
    table = table_ref[...]
    for start in range(0, PAIRS, CHUNK):
        lanes = slice(128 * start, 128 * (start + CHUNK))
        along_x = jnp.dot(pick_ref[...], flat_s[:, lanes], preferred_element_type=F32).astype(BF)
        for slot in range(CAP):
            part = z_stage(along_x[slot * 2 * KXP : (slot + 1) * 2 * KXP], table, 0, CHUNK)
            spectra_out[slot, start * KXP : (start + CHUNK) * KXP, :] = part.astype(BF)


def score_kernel(
    count_ref,
    slot_rot_ref,
    zp_ref,
    x_ref,
    own_ref,
    other_ref,
    table_ref,
    ex_ref,
    wz_ref,
    out_ref,
    pick_s,
    x_s,
    p_s,
    r_s,
    a_s,
):
    slot = pl.program_id(0)

    @pl.when((slot == 0) & (count_ref[0] > 0))
    def _():
        core = lax.axis_index("dom") & 1
        ref_lane = lax.broadcasted_iota(jnp.int32, (1, SEND), 1)
        ref_rot = (ref_lane // PLANES) & (ROT_CLS - 1)
        for to in range(CAP):
            rows = slice(to * 2 * KXP, (to + 1) * 2 * KXP)
            wanted = ref_rot == slot_rot_ref[to]
            pick_s[0, rows] = jnp.where(wanted, x_ref[core], 0.0).astype(BF)
            pick_s[1, rows] = jnp.where(wanted, x_ref[1 - core], 0.0).astype(BF)
        for start in range(0, BOX * BOX, 512):
            lanes = slice(start, start + 512)
            part = jnp.dot(pick_s[0], own_ref[:, lanes], preferred_element_type=F32)
            part = part + jnp.dot(pick_s[1], other_ref[:, lanes], preferred_element_type=F32)
            x_s[:, :, lanes] = part.astype(BF).reshape(CAP, 2 * KXP, 512)

    @pl.when(slot < count_ref[0])
    def _():
        table = table_ref[...]
        xr = x_s.at[slot]
        for start in range(0, PAIRS, STEP):
            part = z_stage(xr, table, start, STEP)
            part = part.astype(BF).astype(F32).reshape(STEP, KXP, 4 * BOX)
            r_s[start : start + STEP] = part[:, :KXV, :]
            mine = zp_ref[start * KXP : (start + STEP) * KXP, :].astype(F32)
            p_s[start : start + STEP] = mine.reshape(STEP, KXP, 4 * BOX)[:, :KXV, :]
        first = lax.broadcasted_iota(jnp.int32, (8, 128), 1) < BOX

        def column(col, carry):
            rows = pl.ds(pl.multiple_of(col * 8, 8), 8)

            def pair(m):
                return r_s[m % PAIRS, rows, 0:128], r_s[m % PAIRS, rows, 128:256]

            def shifted(before, now):
                return tuple(
                    pltpu.roll(jnp.where(first, n, b), BOX, 1) for b, n in zip(before, now)
                )

            def three(re, im):
                return re, im, re - im

            tiles = {m: pair(m) for m in range(-2, 2)}
            even = {m: three(*tiles[m]) for m in range(-1, 2)}
            odd = {m: three(*shifted(tiles[m - 1], tiles[m])) for m in range(-1, 2)}
            last = tiles[1]
            sums = [[jnp.zeros((8, 128), F32) for _ in range(3)] for _ in range(SHIFTS)]
            for j in range(PAIRS):
                new = pair(j + 2)
                even[j + 2] = three(*new)
                odd[j + 2] = three(*shifted(last, new))
                last = new
                pr = p_s[j, rows, 0:128]
                pi = p_s[j, rows, 128:256]
                both = pr + pi
                for u in range(-2, 2):
                    for parity, held in ((0, even), (1, odd)):
                        t = 2 * u + parity + SHIFTS // 2
                        rr, ri, rd = held[j - u]
                        sums[t][0] = sums[t][0] + pr * rr
                        sums[t][1] = sums[t][1] + pi * ri
                        sums[t][2] = sums[t][2] + both * rd
                del even[j - 1], odd[j - 1]
            for t in range(SHIFTS):
                one, two, mix = sums[t]
                a_s[t, rows, 0:128] = one + two
                a_s[t, rows, 128:256] = mix - one + two
            return carry

        lax.fori_loop(0, KXV // 8, column, 0)
        ex = ex_ref[...]
        along_x = [
            jnp.dot(ex, a_s[t].astype(BF), preferred_element_type=F32) for t in range(SHIFTS)
        ]
        cos_rows = jnp.concatenate([u[:SHIFTS] for u in along_x], axis=0).astype(BF)
        sin_rows = jnp.concatenate([u[SHIFTS:] for u in along_x], axis=0).astype(BF)
        both_rows = jnp.concatenate([cos_rows, sin_rows], axis=1)
        final = jnp.dot(both_rows, wz_ref[...], preferred_element_type=F32)
        out_ref[...] = final * (float(BOX) ** -3.5)

    @pl.when(slot >= count_ref[0])
    def _():
        out_ref[...] = jnp.zeros_like(out_ref)


def yz_kernel(parts_ref, z_ref, y_ref, out_ref, z_s, g_s):
    total = parts_ref[0:PER_CHIP].astype(F32)
    for chip in range(1, CHIPS):
        total = total + parts_ref[chip * PER_CHIP : (chip + 1) * PER_CHIP].astype(F32)
    total = total.astype(BF)
    stacked = jnp.concatenate([total[:, 128 * j : 128 * (j + 1)] for j in range(PAIRS)], axis=0)
    z_part = jnp.dot(stacked, z_ref[...], preferred_element_type=F32)
    for j in range(PAIRS):
        for half in range(2):
            start = (2 * j + half) * PER_CHIP
            z_s[start : start + PER_CHIP] = z_part[
                j * PER_CHIP : (j + 1) * PER_CHIP, 128 * half : 128 * (half + 1)
            ]
    by_y = [z_s[pl.ds(n, BOX, stride=PER_CHIP), :].astype(BF) for n in range(PER_CHIP)]
    y_part = jnp.dot(y_ref[...], jnp.concatenate(by_y, axis=1), preferred_element_type=F32)
    first = lax.broadcasted_iota(jnp.int32, (BOX, 128), 1) < BOX
    for n in range(PER_CHIP):
        lanes = slice(128 * n, 128 * (n + 1))
        turned = pltpu.roll(y_part[BOX:, lanes], BOX, 1)
        g_s[pl.ds(n, BOX, stride=PER_CHIP), :] = y_part[:BOX, lanes] + jnp.where(first, turned, -turned)
    out_ref[...] = g_s[...].astype(BF)


def x_rows_kernel(rows_ref, table_hbm, out_ref, table_ref, sem):
    copy = pltpu.make_async_copy(table_hbm, table_ref, sem)
    copy.start()
    copy.wait()
    rows = ROT_CLS * (BOX // DOM)
    first = lax.broadcasted_iota(jnp.int32, (ROT_CLS * BOX, 128), 1) < BOX
    for ky in range(BOX // DOM):
        grid = rows_ref[:, ky * rows : (ky + 1) * rows, :].reshape(ROT_CLS * BOX, 128)
        cos_part = jnp.dot(table_ref[0], grid, preferred_element_type=F32)
        cos_part = cos_part + jnp.dot(table_ref[1], grid, preferred_element_type=F32)
        sin_part = jnp.dot(table_ref[2], grid, preferred_element_type=F32)
        sin_part = sin_part + jnp.dot(table_ref[3], grid, preferred_element_type=F32)
        turned = pltpu.roll(sin_part, BOX, 1)
        total = (cos_part + jnp.where(first, turned, -turned)) * (float(BOX) ** -1.5)
        out_ref[ky] = total.reshape(ROT_CLS, BOX, 128)


VMEM = pl.BlockSpec(memory_space=pltpu.VMEM)
HBM = pl.BlockSpec(memory_space=pltpu.HBM)
SMEM = pl.BlockSpec(memory_space=pltpu.SMEM)


def params(mib):
    return pltpu.CompilerParams(vmem_limit_bytes=mib * 1024 * 1024)


def cost(flops, moved):
    return pl.CostEstimate(flops=flops, bytes_accessed=moved, transcendentals=0)


def shards(particles, references, part_class, part_rot, bucket, bucket_weights, live_count):
    block_size = particles.shape[0]
    voxels = BOX * BOX
    columns = block_size * BOX
    to_other = [(i, i ^ 1) for i in range(DOM)]

    mine_refs = jnp.tile(references.reshape(PER_CHIP, voxels), (CHIPS, 1))

    flat = particles.reshape(columns, voxels)
    classes = part_class.reshape(block_size)
    x_half = x_half_table()
    by_core = x_half.reshape(2 * KXP, CHIPS, 2, 1, PLANES)
    by_core = np.broadcast_to(by_core, (2 * KXP, CHIPS, 2, ROT_CLS, PLANES))
    by_core = by_core.transpose(2, 0, 1, 3, 4).reshape(2, 2 * KXP, SEND)
    held = [
        pltpu.VMEM((columns, voxels), BF),
        pltpu.SemaphoreType.DMA((block_size,)),
    ]

    def whole(*shape):
        return pl.BlockSpec(shape, lambda s: (0,) * len(shape))

    to_send, own, pick, count, slot_rot = pl.pallas_call(
        send_kernel,
        out_shape=(
            jax.ShapeDtypeStruct((SEND, voxels), BF),
            jax.ShapeDtypeStruct((SEND, voxels), BF),
            jax.ShapeDtypeStruct((CAP * 2 * KXP, columns), BF),
            jax.ShapeDtypeStruct((1,), jnp.int32),
            jax.ShapeDtypeStruct((CAP,), jnp.int32),
        ),
        in_specs=[SMEM, SMEM, SMEM, SMEM, VMEM, VMEM, HBM],
        out_specs=(VMEM, VMEM, VMEM, SMEM, SMEM),
        scratch_shapes=[held[0], pltpu.VMEM((2 * SEND, columns), BF), held[1]],
        compiler_params=params(54),
        cost_estimate=cost(1024, 1024),
        name="send",
    )(
        classes,
        part_rot,
        bucket,
        live_count,
        bucket_weights.reshape(1, -1),
        jnp.asarray(np.tile(x_half, (1, block_size)), F32),
        flat,
    )
    to_send, mine_refs = lax.optimization_barrier((to_send, mine_refs))
    other = lax.ppermute(to_send, "dom", to_other)
    refs_own = lax.all_to_all(
        mine_refs, "dom", 0, 0, tiled=True, axis_index_groups=SAME_CORE
    )
    pair_sum = pl.pallas_call(
        pair_kernel,
        out_shape=jax.ShapeDtypeStruct((SEND, voxels), BF),
        in_specs=[VMEM, VMEM],
        out_specs=VMEM,
        compiler_params=params(50),
        cost_estimate=cost(1024, 1024),
        name="pair",
    )(own, other)
    pick, pair_sum = lax.optimization_barrier((pick, pair_sum))
    arrived = lax.all_to_all(pair_sum, "dom", 0, 0, tiled=True, axis_index_groups=SAME_CORE)

    z_table = jnp.asarray(z_complex_table().astype(BF))
    spectra = pl.pallas_call(
        spectra_kernel,
        out_shape=jax.ShapeDtypeStruct((CAP, PAIRS * KXP, 4 * BOX), BF),
        in_specs=[VMEM, HBM, VMEM],
        out_specs=VMEM,
        scratch_shapes=held,
        compiler_params=params(54),
        cost_estimate=cost(1024, 1024),
        name="spectra",
    )(pick, flat, z_table)

    refs_own, spectra = lax.optimization_barrier((refs_own, spectra))
    refs_other = lax.ppermute(refs_own, "dom", to_other)
    ex, wz = shift_tables()

    slots = pl.pallas_call(
        score_kernel,
        out_shape=jax.ShapeDtypeStruct((CAP, SHIFTS * SHIFTS, 128), F32),
        grid=(CAP,),
        in_specs=[
            SMEM,
            SMEM,
            pl.BlockSpec((None, PAIRS * KXP, 4 * BOX), lambda s: (s, 0, 0)),
            whole(2, 2 * KXP, SEND),
            whole(SEND, voxels),
            whole(SEND, voxels),
            whole(4 * BOX, 4 * BOX),
            whole(2 * SHIFTS, KXV),
            whole(8 * BOX, 128),
        ],
        out_specs=pl.BlockSpec((None, SHIFTS * SHIFTS, 128), lambda s: (s, 0, 0)),
        scratch_shapes=[
            pltpu.VMEM((2, CAP * 2 * KXP, SEND), BF),
            pltpu.VMEM((CAP, 2 * KXP, voxels), BF),
            pltpu.VMEM((PAIRS, KXV, 4 * BOX), F32),
            pltpu.VMEM((PAIRS, KXV, 4 * BOX), F32),
            pltpu.VMEM((SHIFTS, KXV, 4 * BOX), F32),
        ],
        compiler_params=params(50),
        cost_estimate=cost(1024, 1024),
        name="slot_scores",
    )(
        count,
        slot_rot,
        spectra,
        jnp.asarray(by_core, F32),
        refs_own,
        refs_other,
        z_table,
        jnp.asarray(ex.astype(BF)),
        jnp.asarray(wz.astype(BF)),
    )
    slot_scores = slots[:, :, :SHIFTS].reshape(CAP, SHIFTS, SHIFTS, SHIFTS)
    slot_scores = slot_scores.transpose(0, 2, 1, 3).reshape(CAP, SHIFTS**3)
    everywhere = lax.all_to_all(jnp.tile(slot_scores, (8, 1)), "rot", 0, 0, tiled=True)
    rows_all = jnp.arange(block_size, dtype=jnp.int32)
    alive = rows_all < live_count[0]
    before = (classes[:, None] == classes[None, :]) & (rows_all[None, :] < rows_all[:, None])
    place = classes * CAP + jnp.sum(before.astype(jnp.int32), axis=1)
    found = (place[:, None] == jnp.arange(8 * CAP, dtype=jnp.int32)[None, :]) & alive[:, None]
    scores = jnp.sum(jnp.where(found[:, :, None], everywhere[None, :, :], 0.0), axis=1)

    z_real = jnp.asarray(z_real_table().astype(BF))
    grids = pl.pallas_call(
        yz_kernel,
        out_shape=jax.ShapeDtypeStruct((BOX * PER_CHIP, 2 * BOX), BF),
        in_specs=[VMEM] * 3,
        out_specs=VMEM,
        scratch_shapes=[pltpu.VMEM((BOX * PER_CHIP, 128), F32)] * 2,
        compiler_params=params(50),
        cost_estimate=cost(1024, 1024),
        name="yz_planes",
    )(arrived, z_real, jnp.asarray(y_table().astype(BF)))
    by_rows = lax.all_to_all(grids, "dom", 0, 0, tiled=True)
    sums = pl.pallas_call(
        x_rows_kernel,
        out_shape=jax.ShapeDtypeStruct((BOX // DOM, ROT_CLS, BOX, 2 * BOX), F32),
        in_specs=[VMEM, HBM],
        out_specs=VMEM,
        scratch_shapes=[
            pltpu.VMEM((4, ROT_CLS * BOX, ROT_CLS * BOX), BF),
            pltpu.SemaphoreType.DMA,
        ],
        compiler_params=params(50),
        name="x_rows",
    )(by_rows.reshape(DOM, PLANES * PER_CHIP, 2 * BOX), jnp.asarray(x_rows_table()))
    return (scores, sums)


def solution(mesh):
    return jax.shard_map(
        shards,
        mesh=mesh,
        in_specs=(
            P("dom", None, None),
            P("rot", "dom", None),
            P("dom", None),
            P("dom"),
            P("dom"),
            P(),
            P("dom"),
        ),
        out_specs=(P("dom", None), P("dom", "rot", None, None)),
        check_vma=False,
    )
```

time: 88.9 us -> 85.3 us (0.960)
  waiting for transfers between devices: 16.4 us -> 26 us
  Pallas kernels: 34.8 us -> 26.5 us
  starting transfers between devices: 27.2 us -> 23.7 us
  local copies, waits for them, and re-layouts: 7.02 us -> 5.94 us
    all_to_all x1, waiting for transfers between devices: 0.01 us -> 6.68 us  [shards(): lax.all_to_all(mine_refs, 'dom', 0, 0, tiled=True, axis_index_groups=SAME...]
    pallas_call x1, Pallas kernels: 6.74 us -> 1.24 us  [shards(): pl.pallas_call(pair_kernel, out_shape=jax.ShapeDtypeStruct((SEND, voxels)...]
    all_to_all x1, waiting for transfers between devices: 4.83 us -> 8.54 us  [shards(): lax.all_to_all(pair_sum, 'dom', 0, 0, tiled=True, axis_index_groups=SAME_...]
    all_to_all x1, starting transfers between devices: 7.06 us -> 3.69 us  [shards(): lax.all_to_all(pair_sum, 'dom', 0, 0, tiled=True, axis_index_groups=SAME_...]
    optimization_barrier x1 -> x0, local copies, waits for them, and re-layouts: 1.32 us -> none  [shards(): mine_refs, part_class = lax.optimization_barrier((mine_refs, part_class))]
    pallas_call x1, Pallas kernels: 9.51 us -> 8.34 us  [shards(): pl.pallas_call(score_kernel, out_shape=jax.ShapeDtypeStruct((CAP, SHIFTS...]
    pallas_call x1, Pallas kernels: 7.08 us -> 5.93 us  [shards(): pl.pallas_call(send_kernel, out_shape=(jax.ShapeDtypeStruct((SEND, voxels...]
    ppermute x1, starting transfers between devices: 0.04 us -> 1.14 us  [shards(): refs_other = lax.ppermute(refs_own, 'dom', to_other)]
  transfers between devices with their start and end apart: 6 -> 6, of which waited for: 3 -> 4; matrix products, arithmetic and copies ran while one was open for 3% -> 1% of each run, Pallas kernels for 30% -> 22%
where the time goes in v3:
time: 85.3 us; the launch traced here: 84.5 us
  Pallas kernels  26.5 us (31%)
  waiting for transfers between devices  26 us (30%)
  starting transfers between devices  23.7 us (28%)
  local copies, waits for them, and re-layouts  5.94 us (7%)
  between operations  1.44 us (2%)
  other arithmetic  1.01 us (1%)
    all_to_all x1, waiting for transfers between devices, shards(): lax.all_to_all(pair_sum, 'dom', 0, 0, tiled=True, axis_index_groups=SAME_...  8.54 us
    pallas_call x1, Pallas kernels, shards(): pl.pallas_call(score_kernel, out_shape=jax.ShapeDtypeStruct((CAP, SHIFTS...  8.34 us
    all_to_all x1, waiting for transfers between devices, shards(): by_rows = lax.all_to_all(grids, 'dom', 0, 0, tiled=True)  7.89 us
    pallas_call x1, Pallas kernels, shards(): pl.pallas_call(spectra_kernel, out_shape=jax.ShapeDtypeStruct((CAP, PAIRS...  7.86 us
    all_to_all x1, starting transfers between devices, shards(): lax.all_to_all(mine_refs, 'dom', 0, 0, tiled=True, axis_index_groups=SAME...  7.75 us
    all_to_all x1, waiting for transfers between devices, shards(): lax.all_to_all(mine_refs, 'dom', 0, 0, tiled=True, axis_index_groups=SAME...  6.68 us
    pallas_call x1, Pallas kernels, shards(): pl.pallas_call(send_kernel, out_shape=(jax.ShapeDtypeStruct((SEND, voxels...  5.93 us
    all_to_all x1, starting transfers between devices, shards(): by_rows = lax.all_to_all(grids, 'dom', 0, 0, tiled=True)  5.57 us
  transfers between devices with their start and end apart: 6, of which 4 were waited for; matrix products, arithmetic and copies ran while one was open for 1% of the time, Pallas kernels for 22%

profile of v3, /device:TPU:1, one launch (start us, length us, event | category | flops | bytes accessed | tf_op | source)
XLA Modules:
  0.0 84.5 jit_solution(8010459622411863695)
XLA Ops:
  1.3 0.9 %tile.18 = bf16[16,4096]{1,0:T(8,128)(2,1)S(1)} reshape(bf16[4,4,4096]{2,1,0:T(4,128)(2,1)} %param.16) | data formatting | bytes 262144 | tf_op jit(solution)/shard_map/tile | solution.py:359
  2.2 5.9 %send.1 = (bf16[128,4096]{1,0:T(8,128)(2,1)}, bf16[128,4096]{1,0:T(8,128)(2,1)}, bf16[384,512]{1,0:T(8,128)(2,1)}, s32[1]{0:T(128)}, s32[4]{0:T(128)}) custom-call(s32[8]{0:T(128)} %bitcast.31, s32[8]{0:T(128)} %rot_ref.1, s32[8]{0:T(128)} %bucket_ref.1, s32[1]{0:T(128)} %copy.21.live_ref, bf16[1,8]{1,0:T(2,128)(2,1)} %bitcast.30, ...), custom_call_target="tpu_custom_call" | custom-call | flops 1024 | bytes 1024 | tf_op jit(solution)/shard_map/send/pallas_call | solution.py:375
  8.2 1.1 %tile.19 = bf16[8,16,4096]{2,1,0:T(8,128)(2,1)} broadcast(bf16[16,4096]{1,0:T(8,128)(2,1)S(1)} %tile.18), dimensions={1,2} | broadcast | bytes 1179648 | tf_op jit(solution)/shard_map/tile | solution.py:359
  9.2 1.4 %collective-permute-start = (bf16[128,4096]{1,0:T(8,128)(2,1)}, bf16[128,4096]{1,0:T(8,128)(2,1)S(1)}, u32[]{:S(2)}, u32[]{:S(2)}) collective-permute-start(bf16[128,4096]{1,0:T(8,128)(2,1)} %get-tuple-element.19), channel_id=1, source_target_pairs={{0,8},{8,0},{16,24},{24,16},{32,40},{40,32},{48,56},{56,48},{64,72... | collective-permute-start | bytes 3145736 | tf_op jit(solution)/shard_map/ppermute | solution.py:400
  10.7 7.7 %all-to-all-start = ((bf16[8,16,4096]{2,1,0:T(8,128)(2,1)}), bf16[8,16,4096]{2,1,0:T(8,128)(2,1)S(1)}, u32[]{:S(2)}, u32[]{:S(2)}) async-start(bf16[8,16,4096]{2,1,0:T(8,128)(2,1)} %bitcast.7), calls=%async_computation | async-start | bytes 2097152 | tf_op jit(solution)/shard_map/all_to_all | solution.py:401
  18.4 0.0 collective-permute-done.other_ref
  18.4 0.0 copy-start
  18.4 1.2 %copy-done = bf16[128,4096]{1,0:T(8,128)(2,1)S(1)} copy-done((bf16[128,4096]{1,0:T(8,128)(2,1)S(1)}, bf16[128,4096]{1,0:T(8,128)(2,1)}, u32[]{:S(2)}) %copy-start) | copy-done | bytes 1048600
  19.6 1.2 %pair.1 = bf16[128,4096]{1,0:T(8,128)(2,1)} custom-call(bf16[128,4096]{1,0:T(8,128)(2,1)S(1)} %copy-done, bf16[128,4096]{1,0:T(8,128)(2,1)S(1)} %collective-permute-done.other_ref), custom_call_target="tpu_custom_call" | custom-call | flops 1024 | bytes 1024 | tf_op jit(solution)/shard_map/pair/pallas_call | solution.py:404
  20.9 0.0 copy-start.7
  20.9 7.9 %spectra.1.zp_ref = bf16[4,1536,256]{2,1,0:T(8,128)(2,1)} custom-call(bf16[384,512]{1,0:T(8,128)(2,1)} %get-tuple-element.20.pick_ref, bf16[512,4096]{1,0:T(8,128)(2,1)} %bitcast.28, bf16[256,256]{1,0:T(8,128)(2,1)} %constant.23.clone.table_ref), custom_call_target="tpu_custom_call" | custom-call | flops 1024 | bytes 1024 | tf_op jit(solution)/shard_map/spectra/pallas_call | solution.py:417
  28.8 6.7 %all-to-all-done = bf16[8,16,4096]{2,1,0:T(8,128)(2,1)S(1)} async-done(((bf16[8,16,4096]{2,1,0:T(8,128)(2,1)}), bf16[8,16,4096]{2,1,0:T(8,128)(2,1)S(1)}, u32[]{:S(2)}, u32[]{:S(2)}) %all-to-all-start) | async-done | bytes 1048608 | tf_op jit(solution)/shard_map/all_to_all | solution.py:401
  35.5 1.1 %collective-permute-start.1 = (bf16[128,4096]{1,0:T(8,128)(2,1)S(1)}, bf16[128,4096]{1,0:T(8,128)(2,1)S(1)}, u32[]{:S(2)}, u32[]{:S(2)}) collective-permute-start(bf16[128,4096]{1,0:T(8,128)(2,1)S(1)} %bitcast.25), channel_id=1, source_target_pairs={{0,8},{8,0},{16,24},{24,16},{32,40},{40,32},{48,56},{56,48},{64,72... | collective-permute-start | bytes 3145736 | tf_op jit(solution)/shard_map/ppermute | solution.py:429
  36.6 3.7 %all-to-all-start.2 = ((bf16[8,16,4096]{2,1,0:T(8,128)(2,1)}), bf16[8,16,4096]{2,1,0:T(8,128)(2,1)S(1)}, u32[]{:S(2)}, u32[]{:S(2)}) async-start(bf16[8,16,4096]{2,1,0:T(8,128)(2,1)} %bitcast.11), calls=%async_computation.2 | async-start | bytes 2097152 | tf_op jit(solution)/shard_map/all_to_all | solution.py:414
  40.3 0.2 convert_reduce_fusion
  40.5 0.0 collective-permute-done.1.other_ref
  40.5 0.0 copy-done.1
  40.6 8.3 %slot_scores.1 = f32[4,64,128]{2,1,0:T(8,128)S(1)} custom-call(s32[1]{0:T(128)} %get-tuple-element.13.count_ref, s32[4]{0:T(128)S(1)} %copy-done.8, bf16[4,1536,256]{2,1,0:T(8,128)(2,1)} %spectra.1.zp_ref, f32[2,96,128]{2,1,0:T(8,128)S(1)} %copy-done.4, bf16[128,4096]{1,0:T(8,128)(2,1)S(1)} %bitcast.26, ...), custom_call_target="tpu_custom_call" | custom-call | flops 1024 | bytes 1024 | tf_op jit(solution)/shard_map/slot_scores/pallas_call | solution.py:432
  49.0 0.1 tile.21
  49.1 8.5 %all-to-all-done.2 = bf16[8,16,4096]{2,1,0:T(8,128)(2,1)S(1)} async-done(((bf16[8,16,4096]{2,1,0:T(8,128)(2,1)}), bf16[8,16,4096]{2,1,0:T(8,128)(2,1)S(1)}, u32[]{:S(2)}, u32[]{:S(2)}) %all-to-all-start.2) | async-done | bytes 1048608 | tf_op jit(solution)/shard_map/all_to_all | solution.py:414
  57.6 0.6 tile.22
  58.2 4.1 %all-to-all-start.1 = ((f32[8,4,512]{2,1,0:T(4,128)}), f32[8,4,512]{2,1,0:T(4,128)S(1)}, u32[]{:S(2)}, u32[]{:S(2)}) async-start(f32[8,4,512]{2,1,0:T(4,128)} %tile.22), calls=%async_computation.1 | async-start | bytes 131072 | tf_op jit(solution)/shard_map/all_to_all | solution.py:471
  62.4 0.0 copy-start.5
  62.4 0.8 copy-done.5
  63.2 1.5 %yz_planes.1 = bf16[1024,128]{1,0:T(8,128)(2,1)} custom-call(bf16[128,4096]{1,0:T(8,128)(2,1)S(1)} %bitcast.24, bf16[128,256]{1,0:T(8,128)(2,1)S(1)} %copy-done.5, bf16[128,64]{1,0:T(8,128)(2,1)S(1)} %copy-done.6), custom_call_target="tpu_custom_call" | custom-call | flops 1024 | bytes 1024 | tf_op jit(solution)/shard_map/yz_planes/pallas_call | solution.py:480
  64.7 2.9 %all-to-all-done.1 = f32[8,4,512]{2,1,0:T(4,128)S(1)} async-done(((f32[8,4,512]{2,1,0:T(4,128)}), f32[8,4,512]{2,1,0:T(4,128)S(1)}, u32[]{:S(2)}, u32[]{:S(2)}) %all-to-all-start.1) | async-done | bytes 65568 | tf_op jit(solution)/shard_map/all_to_all | solution.py:471
  67.6 5.6 %all-to-all-start.3 = ((bf16[16,64,128]{2,1,0:T(8,128)(2,1)}), bf16[16,64,128]{2,1,0:T(8,128)(2,1)S(1)}, u32[]{:S(2)}, u32[]{:S(2)}) async-start(bf16[16,64,128]{2,1,0:T(8,128)(2,1)} %bitcast.13), calls=%async_computation.3 | async-start | bytes 524288 | tf_op jit(solution)/shard_map/all_to_all | solution.py:490
  73.2 0.1 fusion.1
  73.3 0.7 select_reduce_fusion
  74.0 7.9 %all-to-all-done.3.rows_ref = bf16[16,64,128]{2,1,0:T(8,128)(2,1)S(1)} async-done(((bf16[16,64,128]{2,1,0:T(8,128)(2,1)}), bf16[16,64,128]{2,1,0:T(8,128)(2,1)S(1)}, u32[]{:S(2)}, u32[]{:S(2)}) %all-to-all-start.3) | async-done | bytes 262176 | tf_op jit(solution)/shard_map/all_to_all | solution.py:490
  81.9 1.0 %copy-done.2 = bf16[4,256,256]{2,1,0:T(8,128)(2,1)S(1)} copy-done((bf16[4,256,256]{2,1,0:T(8,128)(2,1)S(1)}, bf16[4,256,256]{2,1,0:T(8,128)(2,1)}, u32[]{:S(2)}) %copy-start.2) | copy-done | bytes 524312
  82.9 1.6 %x_rows.1 = f32[4,4,64,128]{3,2,1,0:T(8,128)} custom-call(bf16[16,64,128]{2,1,0:T(8,128)(2,1)S(1)} %all-to-all-done.3.rows_ref, bf16[4,256,256]{2,1,0:T(8,128)(2,1)S(1)} %copy-done.2), custom_call_target="tpu_custom_call" | custom-call | tf_op jit(solution)/shard_map/x_rows/pallas_call | solution.py:491
  (18 shorter events, 0.1 us)
Async XLA Ops:
  9.2 9.2 %collective-permute-start = (bf16[128,4096]{1,0:T(8,128)(2,1)}, bf16[128,4096]{1,0:T(8,128)(2,1)S(1)}, u32[]{:S(2)}, u32[]{:S(2)}) collective-permute-start(bf16[128,4096]{1,0:T(8,128)(2,1)} %get-tuple-element.19), channel_id=1, source_target_pairs={{0,8},{8,0},{16,24},{24,16},{32,40},{40,32},{48,56},{56,48},{64,72... | collective-permute-start | bytes 3145736 | tf_op jit(solution)/shard_map/ppermute | solution.py:400
  10.7 24.8 %all-to-all-start = ((bf16[8,16,4096]{2,1,0:T(8,128)(2,1)}), bf16[8,16,4096]{2,1,0:T(8,128)(2,1)S(1)}, u32[]{:S(2)}, u32[]{:S(2)}) async-start(bf16[8,16,4096]{2,1,0:T(8,128)(2,1)} %bitcast.7), calls=%async_computation | async-start | bytes 2097152 | tf_op jit(solution)/shard_map/all_to_all | solution.py:401
  18.4 1.2 %copy-start = (bf16[128,4096]{1,0:T(8,128)(2,1)S(1)}, bf16[128,4096]{1,0:T(8,128)(2,1)}, u32[]{:S(2)}) copy-start(bf16[128,4096]{1,0:T(8,128)(2,1)} %get-tuple-element.18.own_ref) | copy-start | bytes 3145732
  20.9 19.4 %copy-start.9 = (s32[8,1]{0,1:T(1,128)S(1)}, s32[8,1]{0,1:T(1,128)}, u32[]{:S(2)}) copy-start(s32[8,1]{0,1:T(1,128)} %param.17) | copy-start | bytes 100
  20.9 19.6 %copy-start.1 = (bf16[256,256]{1,0:T(8,128)(2,1)S(1)}, bf16[256,256]{1,0:T(8,128)(2,1)}, u32[]{:S(2)}) copy-start(bf16[256,256]{1,0:T(8,128)(2,1)} %constant.23.clone.table_ref) | copy-start | bytes 393220
  20.9 19.6 %copy-start.3 = (bf16[512,128]{1,0:T(8,128)(2,1)S(1)}, bf16[512,128]{1,0:T(8,128)(2,1)}, u32[]{:S(2)}) copy-start(bf16[512,128]{1,0:T(8,128)(2,1)} %constant.26.clone.wz_ref) | copy-start | bytes 393220
  20.9 19.7 %copy-start.4 = (f32[2,96,128]{2,1,0:T(8,128)S(1)}, f32[2,96,128]{2,1,0:T(8,128)}, u32[]{:S(2)}) copy-start(f32[2,96,128]{2,1,0:T(8,128)} %constant.24.clone.x_ref) | copy-start | bytes 294916
  20.9 19.7 %copy-start.7 = (bf16[16,40]{1,0:T(8,128)(2,1)S(1)}, bf16[16,40]{1,0:T(8,128)(2,1)}, u32[]{:S(2)}) copy-start(bf16[16,40]{1,0:T(8,128)(2,1)} %constant.25.clone.ex_ref) | copy-start | bytes 3844
  20.9 19.7 %copy-start.8 = (s32[4]{0:T(128)S(1)}, s32[4]{0:T(128)}, u32[]{:S(2)}) copy-start(s32[4]{0:T(128)} %get-tuple-element.14.slot_rot_ref) | copy-start | bytes 52
  35.5 5.0 %collective-permute-start.1 = (bf16[128,4096]{1,0:T(8,128)(2,1)S(1)}, bf16[128,4096]{1,0:T(8,128)(2,1)S(1)}, u32[]{:S(2)}, u32[]{:S(2)}) collective-permute-start(bf16[128,4096]{1,0:T(8,128)(2,1)S(1)} %bitcast.25), channel_id=1, source_target_pairs={{0,8},{8,0},{16,24},{24,16},{32,40},{40,32},{48,56},{56,48},{64,72... | collective-permute-start | bytes 3145736 | tf_op jit(solution)/shard_map/ppermute | solution.py:429
  36.6 25.8 %copy-start.6 = (bf16[128,64]{1,0:T(8,128)(2,1)S(1)}, bf16[128,64]{1,0:T(8,128)(2,1)}, u32[]{:S(2)}) copy-start(bf16[128,64]{1,0:T(8,128)(2,1)} %constant.28.clone.y_ref) | copy-start | bytes 49156
  36.6 21.0 %all-to-all-start.2 = ((bf16[8,16,4096]{2,1,0:T(8,128)(2,1)}), bf16[8,16,4096]{2,1,0:T(8,128)(2,1)S(1)}, u32[]{:S(2)}, u32[]{:S(2)}) async-start(bf16[8,16,4096]{2,1,0:T(8,128)(2,1)} %bitcast.11), calls=%async_computation.2 | async-start | bytes 2097152 | tf_op jit(solution)/shard_map/all_to_all | solution.py:414
  58.2 9.3 %all-to-all-start.1 = ((f32[8,4,512]{2,1,0:T(4,128)}), f32[8,4,512]{2,1,0:T(4,128)S(1)}, u32[]{:S(2)}, u32[]{:S(2)}) async-start(f32[8,4,512]{2,1,0:T(4,128)} %tile.22), calls=%async_computation.1 | async-start | bytes 131072 | tf_op jit(solution)/shard_map/all_to_all | solution.py:471
  62.4 0.8 copy-start.5
  67.6 14.3 %all-to-all-start.3 = ((bf16[16,64,128]{2,1,0:T(8,128)(2,1)}), bf16[16,64,128]{2,1,0:T(8,128)(2,1)S(1)}, u32[]{:S(2)}, u32[]{:S(2)}) async-start(bf16[16,64,128]{2,1,0:T(8,128)(2,1)} %bitcast.13), calls=%async_computation.3 | async-start | bytes 524288 | tf_op jit(solution)/shard_map/all_to_all | solution.py:490
  81.9 1.0 %copy-start.2 = (bf16[4,256,256]{2,1,0:T(8,128)(2,1)S(1)}, bf16[4,256,256]{2,1,0:T(8,128)(2,1)}, u32[]{:S(2)}) copy-start(bf16[4,256,256]{2,1,0:T(8,128)(2,1)} %constant.29.clone.table_hbm) | copy-start | bytes 1572868
